TPU v7x, 32 devices: a whole 2x2x4 slice. The times are simulated.
32 devices in a mesh: dp: 8 (over z, x), head: 4 (over y, core).
Axes of the slice: x: 2, y: 2, z: 4, core: 2. Of those that a mesh axis runs over, the one named last changes fastest.
Arguments:
- tokens: bfloat16 [16384, 1024], P(('dp', 'head')), may hold values from -6 to 6
- lengths: int32 [8, 8], P('dp'), may hold values from 1 to 1536, as said below
- attn_gain: float32 [1024], replicated, may hold values from 0.5 to 1.5
- w_query: bfloat16 [1024, 1024], P('dp', 'head'), may hold values from -0.1875 to 0.1875
- w_key: bfloat16 [1024, 1024], P('dp', 'head'), may hold values from -0.1875 to 0.1875
- w_value: bfloat16 [1024, 1024], P('dp', 'head'), may hold values from -0.1875 to 0.1875
- w_beta: bfloat16 [1024, 8], P('dp', 'head'), may hold values from -0.1875 to 0.1875
- w_gate_out: bfloat16 [1024, 1024], P('dp', 'head'), may hold values from -0.1875 to 0.1875
- conv_weight: bfloat16 [3, 4, 1024], P(None, None, 'head'), may hold values from -3 to 3
- head_gain: float32 [128], replicated, may hold values from 0.5 to 1.5
- w_out: bfloat16 [1024, 1024], P('head', 'dp'), may hold values from -0.1875 to 0.1875
- mlp_gain: float32 [1024], replicated, may hold values from 0.5 to 1.5
- w_mlp_gate: bfloat16 [1024, 2816], P('dp', 'head'), may hold values from -0.1875 to 0.1875
- w_mlp_up: bfloat16 [1024, 2816], P('dp', 'head'), may hold values from -0.1875 to 0.1875
- w_down: bfloat16 [2816, 1024], P('head', 'dp'), may hold values from -0.109375 to 0.109375
- cotangent: bfloat16 [16384, 1024], P(('dp', 'head')), may hold values from -6 to 6
Outputs:
- output: bfloat16 [16384, 1024], P(('dp', 'head'))
- input_grad: float32 [16384, 1024], P(('dp', 'head'))
- attn_gain_grad: float32 [1024], replicated
- w_query_grad: float32 [1024, 1024], P('dp', 'head')
- w_key_grad: float32 [1024, 1024], P('dp', 'head')
- w_value_grad: float32 [1024, 1024], P('dp', 'head')
- w_beta_grad: float32 [1024, 8], P('dp', 'head')
- w_gate_out_grad: float32 [1024, 1024], P('dp', 'head')
- conv_grad: float32 [3, 4, 1024], P(None, None, 'head')
- head_gain_grad: float32 [128], replicated
- w_out_grad: float32 [1024, 1024], P('head', 'dp')
- mlp_gain_grad: float32 [1024], replicated
- w_mlp_gate_grad: float32 [1024, 2816], P('dp', 'head')
- w_mlp_up_grad: float32 [1024, 2816], P('dp', 'head')
- w_down_grad: float32 [2816, 1024], P('head', 'dp')
Inputs may be any that keep to these rules, and one draw needn't show every extreme that they name: Each row of lengths sums to 2048; its first entry is at most 256 and its second is 1536.
All inputs are finite; a program needn't handle non-finite values.
Results may differ from a plain program's by a relative error of at most 0.015.
Values may be sent and summed in bfloat16 or wider, within the bound.
A program may use at most 192 MiB of HBM per device.

v0:
```python
from functools import partial

import jax
import jax.numpy as jnp
from jax import lax
from jax.sharding import PartitionSpec as P

HEADS = 8
HEAD_DIM = 128
GROUP = 64
ROW = 2048


HIGH_ACCURACY = lax.Precision.HIGHEST


def scaled_norm(values, norm_weight, epsilon):
    return (
        values
        * lax.rsqrt(jnp.mean(values * values, axis=-1, keepdims=True) + epsilon)
        * norm_weight
    )


def doc_ids(lengths):
    doc_ends = jnp.cumsum(lengths, axis=-1)
    position = jnp.arange(ROW, dtype=jnp.int32)
    return jnp.sum((position[:, None] >= doc_ends[..., None, :]).astype(jnp.int32), axis=-1)


def short_conv(linear, kernel, doc_index):
    conv_width = kernel.shape[0]
    summed = linear * kernel[conv_width - 1]
    for offset in range(1, conv_width):
        shifted = jnp.concatenate(
            [jnp.zeros((offset, linear.shape[1]), linear.dtype), linear[:-offset]], axis=0
        )
        prior_doc = jnp.concatenate(
            [jnp.full((offset,), -1, jnp.int32), doc_index[:-offset]], axis=0
        )
        same_doc = (prior_doc == doc_index).astype(linear.dtype)
        summed = summed + shifted * same_doc[:, None] * kernel[conv_width - 1 - offset]
    return summed


def group_step(carried_state, inputs):
    query_segment, key_segment, value_part, beta_part, doc_part, prior_doc = inputs
    position = jnp.arange(doc_part.shape[0], dtype=jnp.int32)
    same_doc = doc_part[:, None] == doc_part[None, :]
    strict_mask = jnp.logical_and(same_doc, position[:, None] > position[None, :])
    causal_mask = jnp.logical_and(same_doc, position[:, None] >= position[None, :])
    entering_state = (doc_part == prior_doc).astype(query_segment.dtype)
    leaving_state = (doc_part == doc_part[-1]).astype(query_segment.dtype)
    key_gram = jnp.einsum("hik,hjk->hij", key_segment, key_segment, precision=HIGH_ACCURACY)
    coupled = jnp.where(strict_mask, key_gram * beta_part[:, :, None], 0.0)
    targets = jnp.concatenate([key_segment, value_part], axis=2) * beta_part[:, :, None]
    solved = jax.scipy.linalg.solve_triangular(coupled, targets, lower=True, unit_diagonal=True)
    key_dim = key_segment.shape[2]
    key_rows_weighted = solved[:, :, :key_dim]
    value_rows_weighted = solved[:, :, key_dim:]
    corrected_rows = value_rows_weighted - entering_state[None, :, None] * jnp.einsum(
        "nyl,nlm->nym", key_rows_weighted, carried_state, precision=HIGH_ACCURACY
    )
    scores = jnp.where(
        causal_mask,
        jnp.einsum("hik,hjk->hij", query_segment, key_segment, precision=HIGH_ACCURACY),
        0.0,
    )
    layer_output = entering_state[None, :, None] * jnp.einsum(
        "nyl,nlm->nym", query_segment, carried_state, precision=HIGH_ACCURACY
    )
    layer_output = layer_output + jnp.einsum(
        "hij,hjv->hiv", scores, corrected_rows, precision=HIGH_ACCURACY
    )
    updated_state = entering_state[-1] * carried_state + jnp.einsum(
        "lxo,lxb->lob",
        key_segment * leaving_state[None, :, None],
        corrected_rows,
        precision=HIGH_ACCURACY,
    )
    return (updated_state, layer_output)


def delta_row(queries, key_rows, value_rows, beta_rows, doc_index):
    head_count, length, key_dim = queries.shape
    block_count = length // GROUP

    def blocked(stacked):
        return jnp.swapaxes(
            stacked.reshape((head_count, block_count, GROUP) + stacked.shape[2:]), 0, 1
        )

    doc_blocks = doc_index.reshape(block_count, GROUP)
    prior_docs = jnp.concatenate([jnp.full((1,), -1, jnp.int32), doc_blocks[:-1, -1]], axis=0)
    initial = jnp.zeros((head_count, key_dim, value_rows.shape[2]), queries.dtype)
    final_state, outputs = lax.scan(
        jax.checkpoint(group_step),
        initial,
        (
            blocked(queries),
            blocked(key_rows),
            blocked(value_rows),
            blocked(beta_rows),
            doc_blocks,
            prior_docs,
        ),
    )
    return jnp.swapaxes(outputs, 0, 1).reshape(head_count, length, value_rows.shape[2])


def mixer(query_pre, key_pre, value_pre, gate_pre, beta_pre, conv_kernel, head_gain, doc_index):
    head_count = beta_pre.shape[1]
    length = beta_pre.shape[0]

    def prepare(linear, channel, unit_norm):
        activated = jax.nn.silu(short_conv(linear, conv_kernel[channel], doc_index)).reshape(
            length, head_count, HEAD_DIM
        )
        if unit_norm:
            activated = activated * lax.rsqrt(
                jnp.sum(activated * activated, axis=-1, keepdims=True) + 1e-06
            )
        return jnp.swapaxes(activated, 0, 1)

    queries = prepare(query_pre, 0, True) * HEAD_DIM ** (-0.5)
    key_rows = prepare(key_pre, 1, True)
    value_rows = prepare(value_pre, 2, False)
    beta_rows = jnp.swapaxes(jax.nn.sigmoid(beta_pre), 0, 1)
    mixed = delta_row(queries, key_rows, value_rows, beta_rows, doc_index)
    normed = scaled_norm(jnp.swapaxes(mixed, 0, 1), head_gain, 1e-05).reshape(
        length, head_count * HEAD_DIM
    )
    return normed * jax.nn.silu(gate_pre)


def project(left, right):
    return jnp.dot(left, right, preferred_element_type=jnp.float32)


def project_back(grad_rows, weight):
    return lax.dot_general(
        grad_rows, weight, (((1,), (1,)), ((), ())), preferred_element_type=jnp.float32
    )


def outer_grad(input_rows, grad_rows):
    return lax.dot_general(
        input_rows, grad_rows, (((0,), (0,)), ((), ())), preferred_element_type=jnp.float32
    )


def lowered(values):
    return values.astype(jnp.bfloat16)


def on_device(
    tokens,
    lengths,
    attn_gain,
    w_query,
    w_key,
    w_value,
    w_beta,
    w_gate_out,
    conv_weight,
    head_gain,
    w_out,
    mlp_gain,
    w_mlp_gate,
    w_mlp_up,
    w_down,
    cotangent,
):
    sharded = (w_query, w_key, w_value, w_gate_out, w_beta, w_mlp_gate, w_mlp_up, w_out, w_down)
    forward_set = (
        lax.all_gather(sharded[0], "dp", axis=0, tiled=True),
        lax.all_gather(sharded[1], "dp", axis=0, tiled=True),
        lax.all_gather(sharded[2], "dp", axis=0, tiled=True),
        lax.all_gather(sharded[3], "dp", axis=0, tiled=True),
        lax.all_gather(sharded[4], "dp", axis=0, tiled=True),
        lax.all_gather(sharded[5], "dp", axis=0, tiled=True),
        lax.all_gather(sharded[6], "dp", axis=0, tiled=True),
        lax.all_gather(sharded[7], "dp", axis=1, tiled=True),
        lax.all_gather(sharded[8], "dp", axis=1, tiled=True),
    )
    (
        query_full,
        key_full,
        value_full,
        gate_full,
        beta_full,
        inner_gate,
        inner_up,
        out_full,
        down_full,
    ) = forward_set
    doc_index = doc_ids(lengths[0])
    residual_in = tokens.astype(jnp.float32)
    normed, first_pull = jax.vjp(partial(scaled_norm, epsilon=1e-06), residual_in, attn_gain)
    normed_rows = lax.all_gather(lowered(normed), "head", axis=0, tiled=True)
    query_pre = project(normed_rows, query_full)
    key_pre = project(normed_rows, key_full)
    value_pre = project(normed_rows, value_full)
    gate_pre = project(normed_rows, gate_full)
    beta_pre = project(normed_rows, beta_full)
    mixer_local = partial(mixer, doc_index=doc_index)
    mixed, mixer_pull = jax.vjp(
        mixer_local,
        query_pre,
        key_pre,
        value_pre,
        gate_pre,
        beta_pre,
        conv_weight.astype(jnp.float32),
        head_gain,
    )
    mixed_low = lowered(mixed)
    attention = lax.psum_scatter(
        project(mixed_low, out_full), "head", scatter_dimension=0, tiled=True
    )
    hidden_res = residual_in + attention
    second, second_pull = jax.vjp(partial(scaled_norm, epsilon=1e-06), hidden_res, mlp_gain)
    second_rows = lax.all_gather(lowered(second), "head", axis=0, tiled=True)
    ff_gate, ff_up, ff_down = (inner_gate, inner_up, down_full)
    gate_val = project(second_rows, ff_gate)
    up_val = project(second_rows, ff_up)
    sigmoid_gate = jax.nn.sigmoid(gate_val)
    activated = gate_val * sigmoid_gate
    middle = lowered(activated * up_val)
    inner_result = lax.psum_scatter(
        project(middle, ff_down).astype(jnp.bfloat16), "head", scatter_dimension=0, tiled=True
    ).astype(jnp.float32)
    layer_output = (hidden_res + inner_result).astype(jnp.bfloat16)
    backward_set = (
        lax.all_gather(sharded[0], "dp", axis=0, tiled=True),
        lax.all_gather(sharded[1], "dp", axis=0, tiled=True),
        lax.all_gather(sharded[2], "dp", axis=0, tiled=True),
        lax.all_gather(sharded[3], "dp", axis=0, tiled=True),
        lax.all_gather(sharded[4], "dp", axis=0, tiled=True),
        lax.all_gather(sharded[5], "dp", axis=0, tiled=True),
        lax.all_gather(sharded[6], "dp", axis=0, tiled=True),
        lax.all_gather(sharded[7], "dp", axis=1, tiled=True),
        lax.all_gather(sharded[8], "dp", axis=1, tiled=True),
    )
    (
        query_back,
        key_back,
        value_back,
        gate_back,
        beta_back,
        inner_gate_back,
        inner_up_back,
        out_back,
        down_back,
    ) = backward_set
    out_grad = cotangent.astype(jnp.float32)
    grad_rows = lax.all_gather(cotangent, "head", axis=0, tiled=True)
    back_gate, back_up, back_down = (inner_gate_back, inner_up_back, down_back)
    middle_grad = lowered(project_back(grad_rows, back_down)).astype(jnp.float32)
    down_grad = outer_grad(middle, grad_rows)
    up_grad = lowered(middle_grad * activated)
    gate_grad = lowered(
        middle_grad * up_val * sigmoid_gate * (1.0 + gate_val * (1.0 - sigmoid_gate))
    )
    inner_gate_grad = outer_grad(second_rows, gate_grad)
    inner_up_grad = outer_grad(second_rows, up_grad)
    second_terms = project_back(gate_grad, back_gate) + project_back(up_grad, back_up)
    second_grad = lowered(
        lax.psum_scatter(second_terms, "head", scatter_dimension=0, tiled=True)
    ).astype(jnp.float32)
    from_inner, mlp_gain_grad = second_pull(second_grad)
    hidden_grad = out_grad + from_inner
    mixer_grad_rows = lax.all_gather(lowered(hidden_grad), "head", axis=0, tiled=True)
    mixed_grad = lowered(project_back(mixer_grad_rows, out_back)).astype(jnp.float32)
    out_weight_grad = outer_grad(mixed_low, mixer_grad_rows)
    query_grad, key_grad, value_grad, gate_grad_pre, beta_grad, conv_local_grad, head_gain_grad = (
        mixer_pull(mixed_grad)
    )
    query_grad = lowered(query_grad)
    key_grad = lowered(key_grad)
    value_grad = lowered(value_grad)
    gate_grad_pre = lowered(gate_grad_pre)
    beta_grad = lowered(beta_grad)
    query_weight_grad = outer_grad(normed_rows, query_grad)
    key_weight_grad = outer_grad(normed_rows, key_grad)
    value_weight_grad = outer_grad(normed_rows, value_grad)
    gate_weight_grad = outer_grad(normed_rows, gate_grad_pre)
    beta_weight_grad = outer_grad(normed_rows, beta_grad)
    normed_terms = (
        project_back(query_grad, query_back)
        + project_back(key_grad, key_back)
        + project_back(value_grad, value_back)
    )
    normed_terms = (
        normed_terms + project_back(gate_grad_pre, gate_back) + project_back(beta_grad, beta_back)
    )
    normed_grad = lowered(
        lax.psum_scatter(
            normed_terms.astype(jnp.bfloat16), "head", scatter_dimension=0, tiled=True
        ).astype(jnp.float32)
    ).astype(jnp.float32)
    from_mixer, attn_gain_grad = first_pull(normed_grad)
    input_grad = hidden_grad + from_mixer
    local_width = conv_local_grad.shape[2]
    conv_start = lax.axis_index("head") * local_width
    conv_full = jnp.zeros(
        (conv_local_grad.shape[0], conv_local_grad.shape[1], HEADS * HEAD_DIM), jnp.float32
    )
    conv_full = lax.dynamic_update_slice(
        conv_full, conv_local_grad, (jnp.int32(0), jnp.int32(0), conv_start)
    )
    summed_small = lax.psum(
        (attn_gain_grad, mlp_gain_grad, head_gain_grad, conv_full), ("dp", "head")
    )
    conv_grad = lax.dynamic_slice_in_dim(summed_small[3], conv_start, local_width, 2)
    weight_terms = (
        query_weight_grad,
        key_weight_grad,
        value_weight_grad,
        gate_weight_grad,
        beta_weight_grad,
        inner_gate_grad,
        inner_up_grad,
        out_weight_grad,
        down_grad,
    )
    reduced = (
        lax.psum_scatter(weight_terms[0], "dp", scatter_dimension=0, tiled=True),
        lax.psum_scatter(weight_terms[1], "dp", scatter_dimension=0, tiled=True),
        lax.psum_scatter(weight_terms[2], "dp", scatter_dimension=0, tiled=True),
        lax.psum_scatter(weight_terms[3], "dp", scatter_dimension=0, tiled=True),
        lax.psum_scatter(weight_terms[4], "dp", scatter_dimension=0, tiled=True),
        lax.psum_scatter(weight_terms[5], "dp", scatter_dimension=0, tiled=True),
        lax.psum_scatter(weight_terms[6], "dp", scatter_dimension=0, tiled=True),
        lax.psum_scatter(weight_terms[7], "dp", scatter_dimension=1, tiled=True),
        lax.psum_scatter(weight_terms[8], "dp", scatter_dimension=1, tiled=True),
    )
    return (
        layer_output,
        input_grad,
        summed_small[0],
        reduced[0],
        reduced[1],
        reduced[2],
        reduced[4],
        reduced[3],
        conv_grad,
        summed_small[2],
        reduced[7],
        summed_small[1],
        reduced[5],
        reduced[6],
        reduced[8],
    )


def solution(mesh):
    in_specs = (
        P(("dp", "head"), None),
        P("dp", None),
        P(),
        P("dp", "head"),
        P("dp", "head"),
        P("dp", "head"),
        P("dp", "head"),
        P("dp", "head"),
        P(None, None, "head"),
        P(),
        P("head", "dp"),
        P(),
        P("dp", "head"),
        P("dp", "head"),
        P("head", "dp"),
        P(("dp", "head"), None),
    )
    out_specs = (
        P(("dp", "head"), None),
        P(("dp", "head"), None),
        P(),
        P("dp", "head"),
        P("dp", "head"),
        P("dp", "head"),
        P("dp", "head"),
        P("dp", "head"),
        P(None, None, "head"),
        P(),
        P("head", "dp"),
        P(),
        P("dp", "head"),
        P("dp", "head"),
        P("head", "dp"),
    )
    return jax.shard_map(
        on_device, mesh=mesh, in_specs=in_specs, out_specs=out_specs, check_vma=False
    )
```

profile of v0, /device:TPU:0, one launch (start us, length us, event | category | flops | bytes accessed | tf_op | source)
XLA Modules:
  0.0 2889.7 jit_solution(6321862615896675427)
XLA Ops:
  13.8 22.1 all_gather.50
  36.9 33.4 %all_gather.52 = bf16[1024,256]{1,0:T(8,128)(2,1)} all-gather(bf16[128,256]{1,0:T(8,128)(2,1)S(1)} %copy-done.33), channel_id=1, replica_groups=mesh['dp'=8,'head'=4] {'dp'}, dimensions={0}, use_global_device_ids=true | all-gather | bytes 589824 | tf_op jit(solution)/shard_map/all_gather | solution.py:176
  70.3 31.5 %all_gather.49 = bf16[1024,256]{1,0:T(8,128)(2,1)S(1)} all-gather(bf16[128,256]{1,0:T(8,128)(2,1)S(1)} %copy-done.34), channel_id=1, replica_groups=mesh['dp'=8,'head'=4] {'dp'}, dimensions={0}, use_global_device_ids=true | all-gather | bytes 589824 | tf_op jit(solution)/shard_map/all_gather | solution.py:177
  101.8 33.7 %all_gather.51 = bf16[1024,256]{1,0:T(8,128)(2,1)} all-gather(bf16[128,256]{1,0:T(8,128)(2,1)S(1)} %copy-done.35), channel_id=1, replica_groups=mesh['dp'=8,'head'=4] {'dp'}, dimensions={0}, use_global_device_ids=true | all-gather | bytes 589824 | tf_op jit(solution)/shard_map/all_gather | solution.py:178
  135.6 31.6 %all_gather.53 = bf16[1024,256]{1,0:T(8,128)(2,1)S(1)} all-gather(bf16[128,256]{1,0:T(8,128)(2,1)S(1)} %copy-done.36), channel_id=1, replica_groups=mesh['dp'=8,'head'=4] {'dp'}, dimensions={0}, use_global_device_ids=true | all-gather | bytes 589824 | tf_op jit(solution)/shard_map/all_gather | solution.py:179
  167.2 28.1 all_gather.54
  237.2 669.4 %while.40 = (s32[]{:T(128)}, f32[2,128,128]{2,1,0:T(8,128)S(1)}, f32[32,2,64,128]{3,2,0,1:T(8,128)}, f32[32,2,128,128]{3,2,1,0:T(8,128)}, s32[32,64]{1,0:T(8,128...) while((s32[]{:T(128)}, f32[2,128,128]{2,1,0:T(8,128)S(1)}, ...), condition=%wide.region_6.8_spmd.clone, body=%wide.region_5.7_spmd.clone.sunk | while | flops 138830144 | bytes 2356174 | solution.py:96
  327.6 9.8 custom-call.28
  599.5 9.8 custom-call.28
  829.6 9.8 custom-call.28
  927.1 68.1 %reduce-scatter.16.cloned.1.call-done = f32[512,1024]{1,0:T(8,128)} async-done(((f32[2048,1024]{1,0:T(8,128)}), f32[512,1024]{1,0:T(8,128)}) %reduce-scatter.16.cloned.1.call-update) | async-done | bytes 2097168 | tf_op jit(solution)/shard_map/reduce_scatter | solution.py:218
  1000.6 17.1 all-gather.18.cloned.1.call-done
  1025.0 37.7 %all-gather.12.cloned.1.call-done = bf16[1024,704]{0,1:T(8,128)(2,1)} async-done(((bf16[128,704]{0,1:T(8,128)(2,1)}), bf16[1024,704]{0,1:T(8,128)(2,1)}) %all-gather.12.cloned.1.call-update) | async-done | bytes 1441808 | tf_op jit(solution)/shard_map/all_gather | solution.py:181
  1062.7 34.8 %all-gather.10.cloned.1.call-done = bf16[2048,1024]{1,0:T(8,128)(2,1)} async-done(((bf16[512,1024]{1,0:T(8,128)(2,1)}), bf16[2048,1024]{1,0:T(8,128)(2,1)}) %all-gather.10.cloned.1.call-update) | async-done | bytes 4194320 | tf_op jit(solution)/shard_map/all_gather | solution.py:223
  1105.8 37.1 %all-gather.14.cloned.1.call-done = bf16[1024,704]{0,1:T(8,128)(2,1)} async-done(((bf16[128,704]{0,1:T(8,128)(2,1)}), bf16[1024,704]{0,1:T(8,128)(2,1)}) %all-gather.14.cloned.1.call-update) | async-done | bytes 1441808 | tf_op jit(solution)/shard_map/all_gather | solution.py:182
  1142.9 10.9 fusion.77
  1163.4 69.9 %reduce-scatter.20.cloned.1.call-done = f32[512,1024]{1,0:T(8,128)} async-done(((f32[2048,1024]{1,0:T(8,128)}), f32[512,1024]{1,0:T(8,128)}) %reduce-scatter.20.cloned.1.call-update) | async-done | bytes 2097168 | tf_op jit(solution)/shard_map/reduce_scatter | solution.py:269
  1238.7 34.4 %all-gather.20.cloned.1.call-done = bf16[2048,1024]{1,0:T(8,128)(2,1)} async-done(((bf16[512,1024]{1,0:T(8,128)(2,1)}), bf16[2048,1024]{1,0:T(8,128)(2,1)}) %all-gather.20.cloned.1.call-update) | async-done | bytes 4194320 | tf_op jit(solution)/shard_map/all_gather | solution.py:273
  1294.2 852.5 %while.41 = (s32[]{:T(128)}, f32[2,128,128]{2,1,0:T(8,128)S(1)}, f32[32,2,64,128]{3,2,0,1:T(8,128)}, f32[32,2,64,128]{3,2,0,1:T(8,128)}, f32[32,2,64,128]{3,2,0,...) while((s32[]{:T(128)}, f32[2,128,128]{2,1,0:T(8,128)S(1)}, ...), condition=%wide.region_17.19_spmd.clone, body=%wide.region_14.18_spmd.clone.sunk | while | flops 359342272 | bytes 6536971 | solution.py:96
  1329.2 9.8 custom-call.30
  1409.1 9.8 custom-call.30
  2169.4 15.1 multiply_reduce_fusion.6
  2212.2 13.9 add_convert_fusion
  2288.1 40.3 %all-reduce.37 = (f32[1024]{0:T(1024)}, f32[3,4,1024]{2,1,0:T(4,128)S(1)}, f32[128]{0:T(128)}, f32[1024]{0:T(1024)}) all-reduce(f32[1024]{0:T(1024)S(1)} %get-tuple-element.623, f32[3,4,1024]{2,1,0:T(4,128)S(1)} %add_dynamic-update-slice_fusion, f32[128]{0:T(128)S(1)} %get-tuple-element.609, ...), channel_id=1, replica_groups=mesh['dp'=8,'head'=4] {'dp','head'}, use_global_device_ids=true, to_apply=%region_23.25 | all-reduce | flops 14464 | bytes 115712 | tf_op jit(solution)/shard_map/psum | solution.py:312
  2333.4 61.5 %reduce-scatter.38.cloned.1.call-done = f32[704,128]{1,0:T(8,128)} async-done(((f32[704,1024]{1,0:T(8,128)}), f32[704,128]{1,0:T(8,128)}) %reduce-scatter.38.cloned.1.call-update) | async-done | bytes 360464 | tf_op jit(solution)/shard_map/reduce_scatter | solution.py:336
  2395.0 76.2 %reduce-scatter.36.cloned.1.call-done = f32[128,704]{0,1:T(8,128)} async-done(((f32[1024,704]{0,1:T(8,128)}), f32[128,704]{0,1:T(8,128)}) %reduce-scatter.36.cloned.1.call-update) | async-done | bytes 360464 | tf_op jit(solution)/shard_map/reduce_scatter | solution.py:334
  2471.1 76.5 %reduce-scatter.34.cloned.1.call-done = f32[128,704]{0,1:T(8,128)} async-done(((f32[1024,704]{0,1:T(8,128)}), f32[128,704]{0,1:T(8,128)}) %reduce-scatter.34.cloned.1.call-update) | async-done | bytes 360464 | tf_op jit(solution)/shard_map/reduce_scatter | solution.py:333
  2547.6 67.7 %reduce-scatter.32.cloned.1.call-done = f32[256,128]{1,0:T(8,128)} async-done(((f32[256,1024]{1,0:T(8,128)}), f32[256,128]{1,0:T(8,128)}) %reduce-scatter.32.cloned.1.call-update) | async-done | bytes 131088 | tf_op jit(solution)/shard_map/reduce_scatter | solution.py:335
  2615.3 66.5 %reduce-scatter.30.cloned.1.call-done = f32[128,256]{1,0:T(8,128)} async-done(((f32[1024,256]{1,0:T(8,128)}), f32[128,256]{1,0:T(8,128)}) %reduce-scatter.30.cloned.1.call-update) | async-done | bytes 131088 | tf_op jit(solution)/shard_map/reduce_scatter | solution.py:331
  2681.8 66.9 %reduce-scatter.26.cloned.1.call-done = f32[128,256]{1,0:T(8,128)} async-done(((f32[1024,256]{1,0:T(8,128)}), f32[128,256]{1,0:T(8,128)}) %reduce-scatter.26.cloned.1.call-update) | async-done | bytes 131088 | tf_op jit(solution)/shard_map/reduce_scatter | solution.py:329
  2748.7 66.5 %reduce-scatter.24.cloned.1.call-done = f32[128,256]{1,0:T(8,128)} async-done(((f32[1024,256]{1,0:T(8,128)}), f32[128,256]{1,0:T(8,128)}) %reduce-scatter.24.cloned.1.call-update) | async-done | bytes 131088 | tf_op jit(solution)/shard_map/reduce_scatter | solution.py:328
  2815.2 66.9 %reduce-scatter.28.cloned.1.call-done = f32[128,256]{1,0:T(8,128)} async-done(((f32[1024,256]{1,0:T(8,128)}), f32[128,256]{1,0:T(8,128)}) %reduce-scatter.28.cloned.1.call-update) | async-done | bytes 131088 | tf_op jit(solution)/shard_map/reduce_scatter | solution.py:330
  (2127 shorter events, 1706.6 us)
Async XLA Ops:
  8.0 187.3 %all-gather.8.cloned.1.call-start = ((), (), s32[]{:S(2)}) async-start(), calls=%async_computation.13 | async-start | bytes 5242880 | tf_op jit(solution)/shard_map/all_gather | solution.py:200
  10.8 91.0 %copy-start.35 = (bf16[128,256]{1,0:T(8,128)(2,1)S(1)}, bf16[128,256]{1,0:T(8,128)(2,1)}, u32[]{:S(2)}) copy-start(bf16[128,256]{1,0:T(8,128)(2,1)} %param.27) | copy-start | bytes 196612
  10.8 124.7 %copy-start.36 = (bf16[128,256]{1,0:T(8,128)(2,1)S(1)}, bf16[128,256]{1,0:T(8,128)(2,1)}, u32[]{:S(2)}) copy-start(bf16[128,256]{1,0:T(8,128)(2,1)} %param.29) | copy-start | bytes 196612
  13.4 153.8 %copy-start.37 = (bf16[256,128]{1,0:T(8,128)(2,1)S(1)}, bf16[256,128]{1,0:T(8,128)(2,1)}, u32[]{:S(2)}) copy-start(bf16[256,128]{1,0:T(8,128)(2,1)} %param.32) | copy-start | bytes 196612
  13.4 981.8 %reduce-scatter.16.cloned.1.call-start = ((), (), s32[]{:S(2)}) async-start(), calls=%async_computation.14 | async-start | bytes 10485760 | tf_op jit(solution)/shard_map/reduce_scatter | solution.py:218
  35.9 162.7 %copy-start.39 = (bf16[1024,2]{0,1:T(2,128)(2,1)}, bf16[1024,2]{0,1:T(2,128)(2,1)S(1)}, u32[]{:S(2)}) copy-start(bf16[1024,2]{0,1:T(2,128)(2,1)S(1)} %all_gather.50) | copy-start | bytes 12292
  36.7 166.3 %copy-start.48 = (f32[1,1,256]{2,1,0:T(1,128)}, f32[1,1,256]{2,1,0:T(1,128)S(1)}, u32[]{:S(2)}) copy-start(f32[1,1,256]{2,1,0:T(1,128)S(1)} %get-tuple-element.743) | copy-start | bytes 3076
  36.7 166.3 %copy-start.50 = (f32[1,1,256]{2,1,0:T(1,128)}, f32[1,1,256]{2,1,0:T(1,128)S(1)}, u32[]{:S(2)}) copy-start(f32[1,1,256]{2,1,0:T(1,128)S(1)} %get-tuple-element.746) | copy-start | bytes 3076
  36.8 166.3 %copy-start.54 = (f32[1,1,256]{2,1,0:T(1,128)}, f32[1,1,256]{2,1,0:T(1,128)S(1)}, u32[]{:S(2)}) copy-start(f32[1,1,256]{2,1,0:T(1,128)S(1)} %get-tuple-element.744) | copy-start | bytes 3076
  36.8 179.9 %copy-start.46 = (f32[1,1,256]{2,1,0:T(1,128)}, f32[1,1,256]{2,1,0:T(1,128)S(1)}, u32[]{:S(2)}) copy-start(f32[1,1,256]{2,1,0:T(1,128)S(1)} %get-tuple-element.747) | copy-start | bytes 3076
  36.8 179.9 %copy-start.52 = (f32[1,1,256]{2,1,0:T(1,128)}, f32[1,1,256]{2,1,0:T(1,128)S(1)}, u32[]{:S(2)}) copy-start(f32[1,1,256]{2,1,0:T(1,128)S(1)} %get-tuple-element.740) | copy-start | bytes 3076
  36.8 179.8 %copy-start.56 = (f32[1,1,256]{2,1,0:T(1,128)}, f32[1,1,256]{2,1,0:T(1,128)S(1)}, u32[]{:S(2)}) copy-start(f32[1,1,256]{2,1,0:T(1,128)S(1)} %get-tuple-element.748) | copy-start | bytes 3076
  101.8 113.4 %copy-start.24 = (bf16[1024,256]{1,0:T(8,128)(2,1)}, bf16[1024,256]{1,0:T(8,128)(2,1)S(1)}, u32[]{:S(2)}) copy-start(bf16[1024,256]{1,0:T(8,128)(2,1)S(1)} %all_gather.49) | copy-start | bytes 1572868
  167.2 746.7 %copy-start.22 = (bf16[1024,256]{1,0:T(8,128)(2,1)}, bf16[1024,256]{1,0:T(8,128)(2,1)S(1)}, u32[]{:S(2)}) copy-start(bf16[1024,256]{1,0:T(8,128)(2,1)S(1)} %all_gather.53) | copy-start | bytes 1572868
  925.3 75.3 %all-gather.16.cloned.1.call-start = ((), (), s32[]{:S(2)}) async-start(), calls=%async_computation.18 | async-start | bytes 1622016 | tf_op jit(solution)/shard_map/all_gather | solution.py:184
  925.8 91.8 %all-gather.18.cloned.1.call-start = ((), (), s32[]{:S(2)}) async-start(), calls=%async_computation.20 | async-start | bytes 5242880 | tf_op jit(solution)/shard_map/all_gather | solution.py:257
  926.4 136.2 %all-gather.12.cloned.1.call-start = ((), (), s32[]{:S(2)}) async-start(), calls=%async_computation.16 | async-start | bytes 1622016 | tf_op jit(solution)/shard_map/all_gather | solution.py:181
  927.0 170.4 %all-gather.10.cloned.1.call-start = ((), (), s32[]{:S(2)}) async-start(), calls=%async_computation.15 | async-start | bytes 5242880 | tf_op jit(solution)/shard_map/all_gather | solution.py:223
  999.7 143.2 %all-gather.14.cloned.1.call-start = ((), (), s32[]{:S(2)}) async-start(), calls=%async_computation.17 | async-start | bytes 1622016 | tf_op jit(solution)/shard_map/all_gather | solution.py:182
  1000.5 232.8 %reduce-scatter.20.cloned.1.call-start = ((), (), s32[]{:S(2)}) async-start(), calls=%async_computation.21 | async-start | bytes 10485760 | tf_op jit(solution)/shard_map/reduce_scatter | solution.py:269
  1163.3 109.7 %all-gather.20.cloned.1.call-start = ((), (), s32[]{:S(2)}) async-start(), calls=%async_computation.22 | async-start | bytes 5242880 | tf_op jit(solution)/shard_map/all_gather | solution.py:273
  1238.4 1045.9 %reduce-scatter.40.cloned.1.call-start = ((), (), s32[]{:S(2)}) async-start(), calls=%async_computation.32 | async-start | bytes 589824
  2155.3 130.6 %reduce-scatter.22.cloned.1.call-start = ((), (), s32[]{:S(2)}) async-start(), calls=%async_computation.23 | async-start | bytes 5242880 | tf_op jit(solution)/shard_map/reduce_scatter | solution.py:298
  2226.0 102.9 %reduce-scatter.18.cloned.1.call-start = ((), (), s32[]{:S(2)}) async-start(), calls=%async_computation.19 | async-start | bytes 5242880 | tf_op jit(solution)/shard_map/reduce_scatter | solution.py:230
  2233.8 161.2 %reduce-scatter.38.cloned.1.call-start = ((), (), s32[]{:S(2)}) async-start(), calls=%async_computation.31 | async-start | bytes 3244032 | tf_op jit(solution)/shard_map/reduce_scatter | solution.py:336
  2242.6 228.5 %reduce-scatter.36.cloned.1.call-start = ((), (), s32[]{:S(2)}) async-start(), calls=%async_computation.30 | async-start | bytes 3244032 | tf_op jit(solution)/shard_map/reduce_scatter | solution.py:334
  2251.2 296.5 %reduce-scatter.34.cloned.1.call-start = ((), (), s32[]{:S(2)}) async-start(), calls=%async_computation.29 | async-start | bytes 3244032 | tf_op jit(solution)/shard_map/reduce_scatter | solution.py:333
  2259.3 355.9 %reduce-scatter.32.cloned.1.call-start = ((), (), s32[]{:S(2)}) async-start(), calls=%async_computation.28 | async-start | bytes 1179648 | tf_op jit(solution)/shard_map/reduce_scatter | solution.py:335
  2265.0 416.8 %reduce-scatter.30.cloned.1.call-start = ((), (), s32[]{:S(2)}) async-start(), calls=%async_computation.27 | async-start | bytes 1179648 | tf_op jit(solution)/shard_map/reduce_scatter | solution.py:331
  2269.6 479.1 %reduce-scatter.26.cloned.1.call-start = ((), (), s32[]{:S(2)}) async-start(), calls=%async_computation.25 | async-start | bytes 1179648 | tf_op jit(solution)/shard_map/reduce_scatter | solution.py:329
  2274.3 540.9 %reduce-scatter.24.cloned.1.call-start = ((), (), s32[]{:S(2)}) async-start(), calls=%async_computation.24 | async-start | bytes 1179648 | tf_op jit(solution)/shard_map/reduce_scatter | solution.py:328
  2279.0 603.1 %reduce-scatter.28.cloned.1.call-start = ((), (), s32[]{:S(2)}) async-start(), calls=%async_computation.26 | async-start | bytes 1179648 | tf_op jit(solution)/shard_map/reduce_scatter | solution.py:330
  (53 other events, 621.4 us)
Sparse Core Ops, SparseCore 0:
  13.5 37.1 all-gather.7
  925.4 69.7 reduce-scatter.15
  1238.5 34.4 all-gather.19
Sparse Core Ops, SparseCore 1:
  927.8 40.9 all-gather.15
  970.2 47.4 all-gather.17
  1019.5 43.1 all-gather.11
  1064.9 32.5 all-gather.9
  1099.7 43.1 all-gather.13
  1163.4 69.9 reduce-scatter.19
  2155.4 62.0 reduce-scatter.39
  2226.1 44.4 reduce-scatter.21
  2273.0 45.2 reduce-scatter.17
  2322.8 72.1 reduce-scatter.37
  2399.4 71.7 reduce-scatter.35
  2475.7 71.8 reduce-scatter.33
  2551.8 63.4 reduce-scatter.31
  2619.3 62.5 reduce-scatter.29
  2686.2 62.5 reduce-scatter.25
  2752.7 62.4 reduce-scatter.23
  2819.6 62.5 reduce-scatter.27
where the time goes:
time: 2910 us; the launch traced here: 2890 us
  waiting for transfers between devices  850 us (29%)
  other arithmetic  822 us (28%)
  matrix products  563 us (19%)
  local copies, waits for them, and re-layouts  407 us (14%)
  blocking collectives  221 us (8%)
    another operation x224, other arithmetic, group_step(): jax.scipy.linalg.solve_triangular(coupled, targets, lower=True, unit_diag...  635 us
    squeeze x224, local copies, waits for them, and re-layouts, delta_row(): lax.scan(jax.checkpoint(group_step), initial, (blocked(queries), blocked(...  163 us
    dot_general x96, matrix products, group_step(): jnp.einsum('nyl,nlm->nym', query_segment, carried_state, precision=HIGH_A...  82.5 us
    dynamic_slice x64, local copies, waits for them, and re-layouts, delta_row(): lax.scan(jax.checkpoint(group_step), initial, (blocked(queries), blocked(...  79.3 us
    dot_general x128, matrix products, group_step(): jnp.einsum('hik,hjk->hij', query_segment, key_segment, precision=HIGH_ACC...  78.4 us
    reduce_scatter x1, waiting for transfers between devices, on_device(): lax.psum_scatter(weight_terms[5], 'dp', scatter_dimension=0, tiled=True)  76.5 us
    reduce_scatter x1, waiting for transfers between devices, on_device(): lax.psum_scatter(weight_terms[6], 'dp', scatter_dimension=0, tiled=True)  76.2 us
    reduce_scatter x1, waiting for transfers between devices, on_device(): lax.psum_scatter(second_terms, 'head', scatter_dimension=0, tiled=True)  69.9 us
  transfers between devices with their start and end apart: 20, of which 15 were waited for; matrix products, arithmetic and copies ran while one was open for 5% of the time, Pallas kernels for 0%

commit v1 on v0

v1 whole, which is shorter than its diff:
```python
from functools import partial

import jax
import jax.numpy as jnp
from jax import lax
from jax.experimental import pallas as pl
from jax.experimental.pallas import tpu as pltpu
from jax.sharding import PartitionSpec as P

HEAD_DIM = 128
CHUNK = 128
GROUP = 4
STEP = CHUNK * GROUP
PAD = 8
F32 = jnp.float32
BF16 = jnp.bfloat16
VMEM_LIMIT = 56 * 1024 * 1024
SOLVE_PASSES = 1


def dot(left, right, dims):
    return lax.dot_general(left, right, (dims, ((), ())), preferred_element_type=F32)


def mul(left, right):
    return dot(left.astype(BF16), right.astype(BF16), ((1,), (0,)))


def mul_t(left, right):
    return dot(left.astype(BF16), right.astype(BF16), ((1,), (1,)))


def t_mul(left, right):
    return dot(left.astype(BF16), right.astype(BF16), ((0,), (0,)))


def mul_split(left, right):
    lead_l = left.astype(BF16)
    rest_l = (left - lead_l.astype(F32)).astype(BF16)
    lead_r = right.astype(BF16)
    rest_r = (right - lead_r.astype(F32)).astype(BF16)
    dims = ((1,), (0,))
    return dot(lead_l, lead_r, dims) + (dot(rest_l, lead_r, dims) + dot(lead_l, rest_r, dims))


solve_mul = mul if SOLVE_PASSES == 1 else mul_split


def unit_inverses(lowers):
    row = lax.broadcasted_iota(jnp.int32, (CHUNK, CHUNK), 0)
    col = lax.broadcasted_iota(jnp.int32, (CHUNK, CHUNK), 1)
    eye = (row == col).astype(F32)
    level = lambda bit: jnp.logical_and(
        (row >> (bit + 1)) == (col >> (bit + 1)), (row >> bit) > (col >> bit)
    )
    first = level(0)
    solved = [eye - jnp.where(first, a, 0.0) for a in lowers]
    for bit in range(1, CHUNK.bit_length() - 1):
        mask = level(bit)
        right = [solve_mul(jnp.where(mask, a, 0.0), t) for a, t in zip(lowers, solved)]
        solved = [t - solve_mul(t, r) for t, r in zip(solved, right)]
    return solved


def conv_parts(pre, ext, conv, aux):
    summed = pre * conv[3:4, :]
    for offset in range(1, 4):
        shifted = ext[PAD - offset : PAD - offset + STEP, :]
        summed = summed + shifted * aux[:, offset - 1 : offset] * conv[3 - offset : 4 - offset, :]
    return summed


def unit_rows(act, scale):
    out = []
    for h in range(act.shape[1] // HEAD_DIM):
        part = act[:, h * HEAD_DIM : (h + 1) * HEAD_DIM]
        inv = lax.rsqrt(jnp.sum(part * part, axis=-1, keepdims=True) + 1e-6)
        out.append((part * inv * scale, inv))
    return out


def chunk_masks(aux, docrow):
    row = lax.broadcasted_iota(jnp.int32, (CHUNK, CHUNK), 0)
    col = lax.broadcasted_iota(jnp.int32, (CHUNK, CHUNK), 1)
    made = []
    for c in range(GROUP):
        same = aux[c * CHUNK : (c + 1) * CHUNK, 8:9] == docrow[c : c + 1, :]
        made.append((jnp.logical_and(same, row > col), jnp.logical_and(same, row >= col)))
    return made


def mixer_fwd_kernel(
    x_ref, w_ref, aux_ref, docrow_ref, conv_ref, gain_ref,
    pre_ref, mixed_ref, o_ref, t_ref, phi_ref, s_ref, p_ref, d_ref, ew_ref,
    ext, state,
):
    heads = mixed_ref.shape[1] // HEAD_DIM
    hid = heads * HEAD_DIM

    @pl.when(pl.program_id(0) == 0)
    def _():
        ext[0:PAD, :] = jnp.zeros((PAD, 3 * hid), F32)
        state[...] = jnp.zeros_like(state)

    pre_ref[...] = dot(x_ref[...], w_ref[...], ((1,), (0,)))
    aux = aux_ref[...]
    conv = conv_ref[...]
    pre = pre_ref[:, : 3 * hid]
    ext[PAD:, :] = pre
    act = conv_parts(pre, ext, conv, aux)
    act = act * jax.nn.sigmoid(act)
    ext[0:PAD, :] = ext[STEP:, :]
    q = unit_rows(act[:, :hid], HEAD_DIM**-0.5)
    k = unit_rows(act[:, hid : 2 * hid], 1.0)
    beta = jax.nn.sigmoid(pre_ref[:, 4 * hid : 4 * hid + 8])
    masks = chunk_masks(aux, docrow_ref[0])

    items = [(c, h) for c in range(GROUP) for h in range(heads)]
    rows = [slice(c * CHUNK, (c + 1) * CHUNK) for c in range(GROUP)]
    lowers, scores = [], []
    for c, h in items:
        key, query = k[h][0][rows[c]], q[h][0][rows[c]]
        both = mul_t(jnp.concatenate([key, query], axis=0), key)
        lowers.append(jnp.where(masks[c][0], both[:CHUNK] * beta[rows[c], h : h + 1], 0.0))
        scores.append(jnp.where(masks[c][1], both[CHUNK:], 0.0).astype(BF16))
    solved = unit_inverses(lowers)
    parts = []
    for (c, h), inverse, score in zip(items, solved, scores):
        key = k[h][0][rows[c]]
        value = act[rows[c], 2 * hid + h * HEAD_DIM : 2 * hid + (h + 1) * HEAD_DIM]
        b = beta[rows[c], h : h + 1]
        enter, leave = aux[rows[c], 3:4], aux[rows[c], 4:5]
        inverse = inverse.astype(BF16)
        wu = mul(inverse, jnp.concatenate([key * b, value * b], axis=1))
        ew, u = wu[:, :HEAD_DIM] * enter, wu[:, HEAD_DIM:]
        phi_b = t_mul(key * leave, jnp.concatenate([ew, u], axis=1))
        parts.append((ew, u, phi_b[:, :HEAD_DIM].astype(BF16), phi_b[:, HEAD_DIM:]))
        t_ref[c, h] = inverse
        p_ref[c, h] = score
        ew_ref[c, h] = ew.astype(BF16)
        phi_ref[c, h] = parts[-1][2]
    for h in range(heads):
        s = state[h]
        for c in range(GROUP):
            low = s.astype(BF16)
            s_ref[c, h] = low
            _, _, phi, b_term = parts[c * heads + h]
            keep = aux[(c + 1) * CHUNK - 1 : (c + 1) * CHUNK, 3:4]
            s = s * keep - mul(phi, low) + b_term
        state[h] = s
    gain = gain_ref[...]
    for (c, h), (ew, u, _, _), score in zip(items, parts, scores):
        enter = aux[rows[c], 3:4]
        from_state = mul(jnp.concatenate([ew, q[h][0][rows[c]] * enter], axis=0), s_ref[c, h])
        d = (u - from_state[:CHUNK]).astype(BF16)
        d_ref[c, h] = d
        o = from_state[CHUNK:] + mul(score, d)
        cols = slice(h * HEAD_DIM, (h + 1) * HEAD_DIM)
        o_ref[rows[c], cols] = o
        normed = o * lax.rsqrt(jnp.mean(o * o, axis=-1, keepdims=True) + 1e-5) * gain
        gate = pre_ref[rows[c], 3 * hid + h * HEAD_DIM : 3 * hid + (h + 1) * HEAD_DIM]
        mixed_ref[rows[c], cols] = (normed * (gate * jax.nn.sigmoid(gate))).astype(BF16)


def mixer_bwd_kernel(
    hg_ref, wout_ref, pre_ref, halo_ref, aux_ref, docrow_ref, conv_ref, gain_ref,
    o_ref, t_ref, phi_ref, s_ref, p_ref, d_ref, ew_ref,
    dpre_ref, dconv_ref, dgain_ref,
    ext, later, dstate,
):
    heads = o_ref.shape[1] // HEAD_DIM
    hid = heads * HEAD_DIM

    @pl.when(pl.program_id(0) == 0)
    def _():
        later[STEP:, :] = jnp.zeros((PAD, 3 * hid), F32)
        dstate[...] = jnp.zeros_like(dstate)
        dconv_ref[...] = jnp.zeros_like(dconv_ref)
        dgain_ref[...] = jnp.zeros_like(dgain_ref)

    mixed_grad = dot(hg_ref[...], wout_ref[...], ((1,), (0,))).astype(BF16).astype(F32)
    aux = aux_ref[...]
    conv = conv_ref[...]
    pre = pre_ref[:, : 3 * hid]
    ext[0:PAD, :] = halo_ref[:, : 3 * hid]
    ext[PAD:, :] = pre
    lin = conv_parts(pre, ext, conv, aux)
    sig = jax.nn.sigmoid(lin)
    act = lin * sig
    dsilu = sig * (1.0 + lin * (1.0 - sig))
    scale = HEAD_DIM**-0.5
    q = unit_rows(act[:, :hid], 1.0)
    k = unit_rows(act[:, hid : 2 * hid], 1.0)
    beta = jax.nn.sigmoid(pre_ref[:, 4 * hid : 4 * hid + 8])
    masks = chunk_masks(aux, docrow_ref[0])
    gain = gain_ref[...]

    items = [(c, h) for c in range(GROUP) for h in range(heads)]
    rows = [slice(c * CHUNK, (c + 1) * CHUNK) for c in range(GROUP)]
    cols = [slice(h * HEAD_DIM, (h + 1) * HEAD_DIM) for h in range(heads)]

    d_out, d_gain = [], jnp.zeros((1, HEAD_DIM), F32)
    for h in range(heads):
        o = o_ref[:, cols[h]]
        inv = lax.rsqrt(jnp.mean(o * o, axis=-1, keepdims=True) + 1e-5)
        unit = o * inv
        gate = pre_ref[:, 3 * hid + h * HEAD_DIM : 3 * hid + (h + 1) * HEAD_DIM]
        s = jax.nn.sigmoid(gate)
        dm = mixed_grad[:, cols[h]]
        dpre_ref[:, 3 * hid + h * HEAD_DIM : 3 * hid + (h + 1) * HEAD_DIM] = (
            dm * unit * gain * (s * (1.0 + gate * (1.0 - s)))
        ).astype(BF16)
        dn = dm * (gate * s)
        d_gain = d_gain + jnp.sum(dn * unit, axis=0, keepdims=True)
        du = dn * gain
        d_out.append(inv * (du - unit * jnp.mean(du * unit, axis=-1, keepdims=True)))
    dgain_ref[...] += d_gain

    first = []
    for c, h in items:
        enter = aux[rows[c], 3:4]
        do = d_out[h][rows[c]].astype(BF16)
        eq = (q[h][0][rows[c]] * (enter * scale)).astype(BF16)
        x = t_mul(p_ref[c, h], do)
        c_term = t_mul(
            jnp.concatenate([eq, -ew_ref[c, h]], axis=0),
            jnp.concatenate([do, x.astype(BF16)], axis=0),
        )
        first.append((do, x, c_term))
    after = {}
    for h in range(heads):
        ds = dstate[h]
        for c in reversed(range(GROUP)):
            low = ds.astype(BF16)
            after[c, h] = low
            keep = aux[(c + 1) * CHUNK - 1 : (c + 1) * CHUNK, 3:4]
            ds = ds * keep - t_mul(phi_ref[c, h], low) + first[c * heads + h][2]
        dstate[h] = ds
    db_cols = []
    grads = {}
    for (c, h), (do, x, _) in zip(items, first):
        enter, leave = aux[rows[c], 3:4], aux[rows[c], 4:5]
        b = beta[rows[c], h : h + 1]
        key, query = k[h][0][rows[c]], q[h][0][rows[c]] * scale
        value = act[rows[c], 2 * hid + h * HEAD_DIM : 2 * hid + (h + 1) * HEAD_DIM]
        ds = after[c, h]
        d, s = d_ref[c, h], s_ref[c, h]
        dr = t_mul(t_ref[c, h], x + mul(key * leave, ds))
        stacked = jnp.concatenate([do, dr.astype(BF16)], axis=0)
        with_d = mul_t(stacked, d)
        with_s = mul_t(stacked, s) * jnp.concatenate([enter, enter], axis=0)
        dp = jnp.where(masks[c][1], with_d[:CHUNK], 0.0)
        da = jnp.where(masks[c][0], -with_d[CHUNK:], 0.0)
        pair = jnp.concatenate([dp, da], axis=0).astype(BF16)
        with_k = mul(pair, key)
        dq = with_s[:CHUNK] + with_k[:CHUNK]
        row_k = with_k[CHUNK:] - with_s[CHUNK:]
        dk = b * row_k + t_mul(pair, jnp.concatenate([query, key * b], axis=0))
        dk = dk + mul_t(d, ds) * leave
        db = jnp.sum(dr * value + key * row_k, axis=-1, keepdims=True)
        grads[c, h] = (dq * scale, dk, dr * b, db * b * (1.0 - b))
    for h in range(heads):
        whole = [jnp.concatenate([grads[c, h][i] for c in range(GROUP)], axis=0) for i in range(4)]
        for i, unit in ((0, q[h]), (1, k[h])):
            y, inv = unit
            grad = inv * (whole[i] - y * jnp.sum(y * whole[i], axis=-1, keepdims=True))
            at = slice(i * hid + h * HEAD_DIM, i * hid + (h + 1) * HEAD_DIM)
            later[0:STEP, at] = grad * dsilu[:, at]
        at = slice(2 * hid + h * HEAD_DIM, 2 * hid + (h + 1) * HEAD_DIM)
        later[0:STEP, at] = whole[2] * dsilu[:, at]
        db_cols.append(whole[3])
    lane = lax.broadcasted_iota(jnp.int32, (STEP, HEAD_DIM), 1)
    tail = jnp.zeros((STEP, HEAD_DIM), F32)
    for h in range(heads):
        tail = jnp.where(lane == h, db_cols[h], tail)
    dpre_ref[:, 4 * hid :] = tail.astype(BF16)
    dlin = later[0:STEP, :]
    dpre = dlin * conv[3:4, :]
    taps = [jnp.sum(dlin * pre, axis=0, keepdims=True)]
    for offset in range(1, 4):
        ahead = later[offset : offset + STEP, :]
        dpre = dpre + ahead * aux[:, 4 + offset : 5 + offset] * conv[3 - offset : 4 - offset, :]
        behind = ext[PAD - offset : PAD - offset + STEP, :] * aux[:, offset - 1 : offset]
        taps.append(jnp.sum(dlin * behind, axis=0, keepdims=True))
    dpre_ref[:, : 3 * hid] = dpre.astype(BF16)
    for offset in range(4):
        dconv_ref[3 - offset : 4 - offset, :] += taps[offset]
    later[STEP:, :] = later[0:PAD, :]


def mixer_fwd(x_rows, weights, aux, docrow, conv, gain):
    length, width = x_rows.shape[0], weights.shape[1]
    hid = conv.shape[1] // 3
    heads, chunks = hid // HEAD_DIM, length // CHUNK
    rows = lambda n: pl.BlockSpec((STEP, n), lambda i: (i, 0))
    whole = lambda a: pl.BlockSpec(a.shape, lambda i: (0,) * a.ndim)
    square = pl.BlockSpec((GROUP, heads, CHUNK, HEAD_DIM), lambda i: (i, 0, 0, 0))
    squares = jax.ShapeDtypeStruct((chunks, heads, CHUNK, HEAD_DIM), BF16)
    return pl.pallas_call(
        mixer_fwd_kernel,
        grid=(length // STEP,),
        in_specs=[
            rows(x_rows.shape[1]), whole(weights), rows(aux.shape[1]),
            pl.BlockSpec((1, GROUP, CHUNK), lambda i: (i, 0, 0)), whole(conv), whole(gain),
        ],
        out_specs=[rows(width), rows(hid), rows(hid)] + [square] * 6,
        out_shape=[
            jax.ShapeDtypeStruct((length, width), F32),
            jax.ShapeDtypeStruct((length, hid), BF16),
            jax.ShapeDtypeStruct((length, hid), F32),
        ]
        + [squares] * 6,
        scratch_shapes=[
            pltpu.VMEM((PAD + STEP, 3 * hid), F32),
            pltpu.VMEM((heads, HEAD_DIM, HEAD_DIM), F32),
        ],
        compiler_params=pltpu.CompilerParams(vmem_limit_bytes=VMEM_LIMIT),
        name="mixer_fwd",
    )(x_rows, weights, aux, docrow, conv, gain)


def mixer_bwd(hg_rows, out_t, aux, docrow, conv, gain, saved):
    pre, o, t, phi, s, p, d, ew = saved
    length, width = pre.shape
    hid = conv.shape[1] // 3
    heads, steps = hid // HEAD_DIM, length // STEP
    last = steps - 1
    rows = lambda n: pl.BlockSpec((STEP, n), lambda i: (last - i, 0))
    whole = lambda a: pl.BlockSpec(a.shape, lambda i: (0,) * a.ndim)
    square = pl.BlockSpec((GROUP, heads, CHUNK, HEAD_DIM), lambda i: (last - i, 0, 0, 0))
    halo = pl.BlockSpec(
        (PAD, width), lambda i: (jnp.maximum((last - i) * (STEP // PAD) - 1, 0), 0)
    )
    return pl.pallas_call(
        mixer_bwd_kernel,
        grid=(steps,),
        in_specs=[
            rows(hg_rows.shape[1]), whole(out_t), rows(width), halo, rows(aux.shape[1]),
            pl.BlockSpec((1, GROUP, CHUNK), lambda i: (last - i, 0, 0)), whole(conv), whole(gain),
            rows(hid),
        ]
        + [square] * 6,
        out_specs=[
            rows(width),
            pl.BlockSpec((4, 3 * hid), lambda i: (0, 0)),
            pl.BlockSpec((1, HEAD_DIM), lambda i: (0, 0)),
        ],
        out_shape=[
            jax.ShapeDtypeStruct((length, width), BF16),
            jax.ShapeDtypeStruct((4, 3 * hid), F32),
            jax.ShapeDtypeStruct((1, HEAD_DIM), F32),
        ],
        scratch_shapes=[
            pltpu.VMEM((PAD + STEP, 3 * hid), F32),
            pltpu.VMEM((STEP + PAD, 3 * hid), F32),
            pltpu.VMEM((heads, HEAD_DIM, HEAD_DIM), F32),
        ],
        compiler_params=pltpu.CompilerParams(vmem_limit_bytes=VMEM_LIMIT),
        name="mixer_bwd",
    )(hg_rows, out_t, pre, pre, aux, docrow, conv, gain, o, t, phi, s, p, d, ew)


def doc_tables(lengths, length):
    count = lengths.shape[0]
    index = jnp.arange(count)
    ends = jnp.sum(jnp.where(index[None, :] <= index[:, None], lengths[None, :], 0), axis=1)
    position = jnp.arange(length, dtype=jnp.int32)
    doc = jnp.sum((position[:, None] >= ends[None, :]).astype(jnp.int32), axis=1)
    no_doc = lambda n: jnp.full((n,), -1, jnp.int32)
    before = [jnp.concatenate([no_doc(o), doc[:-o]]) == doc for o in (1, 2, 3)]
    after = [jnp.concatenate([doc[o:], no_doc(o)]) == doc for o in (1, 2, 3)]
    blocks = doc.reshape(-1, CHUNK)
    ending = blocks[:, -1:]
    prior = jnp.concatenate([no_doc(1)[:, None], ending[:-1]], axis=0)
    enter = (blocks == prior).reshape(-1)
    leave = (blocks == ending).reshape(-1)
    columns = before + [enter, leave] + after + [doc]
    aux = jnp.stack([c.astype(F32) for c in columns], axis=1)
    return aux, doc.astype(F32).reshape(-1, GROUP, CHUNK)


def low(values):
    return values.astype(BF16)


def inverse_rms(values):
    return lax.rsqrt(jnp.mean(values * values, axis=-1, keepdims=True) + 1e-6)


def norm_back(grad, values, inverse, gain):
    scaled = grad * gain
    mean = jnp.mean(scaled * values, axis=-1, keepdims=True)
    into = inverse * scaled - values * (inverse * inverse * inverse) * mean
    return into, jnp.sum(grad * values * inverse, axis=0)


def gather_rows(values):
    return lax.all_gather(values, "head", axis=0, tiled=True)


def scatter_rows(values):
    return lax.psum_scatter(low(values), "head", scatter_dimension=0, tiled=True).astype(F32)


def on_device(
    tokens,
    lengths,
    attn_gain,
    w_query,
    w_key,
    w_value,
    w_beta,
    w_gate_out,
    conv_weight,
    head_gain,
    w_out,
    mlp_gain,
    w_mlp_gate,
    w_mlp_up,
    w_down,
    cotangent,
):
    hid, heads, ff = w_query.shape[1], w_beta.shape[1], w_mlp_gate.shape[1]
    beta_wide = jnp.pad(w_beta, ((0, 0), (0, HEAD_DIM - heads)))
    mine = jnp.concatenate([w_query, w_key, w_value, w_gate_out, beta_wide, w_out.T], axis=1)
    first_set = lax.all_gather(mine, "dp", axis=0, tiled=True)
    mine = jnp.concatenate([w_mlp_gate, w_mlp_up, w_down.T], axis=1)
    second_set = lax.all_gather(mine, "dp", axis=0, tiled=True)
    mix_width = 4 * hid + HEAD_DIM
    w_mix, out_t = first_set[:, :mix_width], first_set[:, mix_width:]
    w_ff, down_t = second_set[:, : 2 * ff], second_set[:, 2 * ff :]

    x = tokens.astype(F32)
    x_inv = inverse_rms(x)
    normed_rows = gather_rows(low(x * x_inv * attn_gain))
    length = normed_rows.shape[0]
    aux, docrow = doc_tables(lengths[0], length)
    conv = jnp.swapaxes(conv_weight.astype(F32), 0, 1).reshape(conv_weight.shape[1], 3 * hid)
    gain = head_gain[None, :]
    pre, mixed, *saved = mixer_fwd(normed_rows, w_mix, aux, docrow, conv, gain)
    attention = scatter_rows(dot(mixed, out_t, ((1,), (1,))))
    hidden = x + attention
    h_inv = inverse_rms(hidden)
    second_rows = gather_rows(low(hidden * h_inv * mlp_gain))
    both = dot(second_rows, w_ff, ((1,), (0,)))
    gate, up = both[:, :ff], both[:, ff:]
    sig = jax.nn.sigmoid(gate)
    activated = gate * sig
    middle = low(activated * up)
    output = low(hidden + scatter_rows(dot(middle, down_t, ((1,), (1,)))))

    cot_rows = gather_rows(cotangent)
    middle_grad = low(dot(cot_rows, down_t, ((1,), (0,)))).astype(F32)
    up_grad = low(middle_grad * activated)
    gate_grad = low(middle_grad * up * sig * (1.0 + gate * (1.0 - sig)))
    ff_grad = jnp.concatenate([gate_grad, up_grad], axis=1)
    outer = lambda left, right: dot(left, right, ((0,), (0,)))
    second_grad = low(scatter_rows(dot(ff_grad, w_ff, ((1,), (1,))))).astype(F32)
    mlp_terms = jnp.concatenate(
        [low(outer(second_rows, ff_grad)), low(outer(cot_rows, middle))], axis=1
    )
    mlp_reduced = lax.psum_scatter(mlp_terms, "dp", scatter_dimension=0, tiled=True).astype(F32)
    from_mlp, mlp_gain_grad = norm_back(second_grad, hidden, h_inv, mlp_gain)
    hidden_grad = cotangent.astype(F32) + from_mlp
    hg_rows = gather_rows(low(hidden_grad))
    dpre, conv_part, head_gain_grad = mixer_bwd(
        hg_rows, out_t, aux, docrow, conv, gain, (pre, *saved)
    )
    normed_grad = low(scatter_rows(dot(dpre, w_mix, ((1,), (1,))))).astype(F32)
    mix_terms = jnp.concatenate(
        [low(outer(normed_rows, dpre)), low(outer(hg_rows, mixed))], axis=1
    )
    mix_reduced = lax.psum_scatter(mix_terms, "dp", scatter_dimension=0, tiled=True).astype(F32)
    from_mixer, attn_gain_grad = norm_back(normed_grad, x, x_inv, attn_gain)
    input_grad = hidden_grad + from_mixer

    taps = conv_part.shape[0]
    conv_local = jnp.swapaxes(conv_part.reshape(taps, 3, hid), 0, 1)
    start = lax.axis_index("head") * hid
    conv_full = jnp.zeros((3, taps, hid * lax.axis_size("head")), F32)
    conv_full = lax.dynamic_update_slice(conv_full, conv_local, (0, 0, start))
    summed = lax.psum((attn_gain_grad, mlp_gain_grad, head_gain_grad[0], conv_full), ("dp", "head"))
    conv_grad = lax.dynamic_slice_in_dim(summed[3], start, hid, 2)
    part = lambda i: mix_reduced[:, i * hid : (i + 1) * hid]
    return (
        output,
        input_grad,
        summed[0],
        part(0),
        part(1),
        part(2),
        mix_reduced[:, 4 * hid : 4 * hid + heads],
        part(3),
        conv_grad,
        summed[2],
        mix_reduced[:, mix_width:].T,
        summed[1],
        mlp_reduced[:, :ff],
        mlp_reduced[:, ff : 2 * ff],
        mlp_reduced[:, 2 * ff :].T,
    )


def solution(mesh):
    rows = P(("dp", "head"), None)
    in_specs = (
        rows,
        P("dp", None),
        P(),
        P("dp", "head"),
        P("dp", "head"),
        P("dp", "head"),
        P("dp", "head"),
        P("dp", "head"),
        P(None, None, "head"),
        P(),
        P("head", "dp"),
        P(),
        P("dp", "head"),
        P("dp", "head"),
        P("head", "dp"),
        rows,
    )
    out_specs = (
        rows,
        rows,
        P(),
        P("dp", "head"),
        P("dp", "head"),
        P("dp", "head"),
        P("dp", "head"),
        P("dp", "head"),
        P(None, None, "head"),
        P(),
        P("head", "dp"),
        P(),
        P("dp", "head"),
        P("dp", "head"),
        P("head", "dp"),
    )
    return jax.shard_map(
        on_device, mesh=mesh, in_specs=in_specs, out_specs=out_specs, check_vma=False
    )
```

time: 2910 us -> 725 us (0.25)
  other arithmetic: 822 us -> 28 us
  matrix products: 563 us -> 80.5 us
  waiting for transfers between devices: 850 us -> 447 us
  local copies, waits for them, and re-layouts: 407 us -> 31.8 us
  blocking collectives: 221 us -> 40.5 us
  Pallas kernels: 0 us -> 73.1 us
    another operation x257 -> x1, other arithmetic: 636 us -> 0.08 us  [doc_tables(): aux = jnp.stack([c.astype(F32) for c in columns], axis=1)]
    reduce_scatter x12 -> x6, waiting for transfers between devices: 687 us -> 221 us  [the longest x4 133 us: scatter_rows(): lax.psum_scatter(low(values), 'head', scatter_dimension=0, tiled=True)]
    dot_general x730 -> x10, matrix products: 517 us -> 80.5 us  [dot(): lax.dot_general(left, right, (dims, ((), ())), preferred_element_type=F32)]
    all_gather x6 -> x0, blocking collectives: 180 us -> none  [the longest x1 33.7 us: on_device(): lax.all_gather(sharded[2], 'dp', axis=0, tiled=True)]
    squeeze x224 -> x0, local copies, waits for them, and re-layouts: 163 us -> none  [delta_row(): lax.scan(jax.checkpoint(group_step), initial, (blocked(queries), blocked(...]
    convert_element_type x103 -> x8, other arithmetic: 91.3 us -> 9.28 us  [the longest x3 6.42 us: low(): return values.astype(BF16)]
    dynamic_slice x65 -> x1, local copies, waits for them, and re-layouts: 79.9 us -> 0.6 us  [on_device(): conv_grad = lax.dynamic_slice_in_dim(summed[3], start, hid, 2)]
    pallas_call x0 -> x2, Pallas kernels: none -> 73.1 us  [the longest x1 45.5 us: mixer_bwd(): pl.pallas_call(mixer_bwd_kernel, grid=(steps,), in_specs=[rows(hg_rows.sh...]
  transfers between devices with their start and end apart: 20 -> 12, of which waited for: 15 -> 12; matrix products, arithmetic and copies ran while one was open for 5% -> 13% of each run, Pallas kernels for 0% -> 6%
where the time goes in v1:
time: 725 us; the launch traced here: 717 us
  waiting for transfers between devices  447 us (62%)
  matrix products  80.5 us (11%)
  Pallas kernels  73.1 us (10%)
  blocking collectives  40.5 us (6%)
  local copies, waits for them, and re-layouts  31.8 us (4%)
  other arithmetic  28 us (4%)
  between operations  14.7 us (2%)
    reduce_scatter x4, waiting for transfers between devices, scatter_rows(): lax.psum_scatter(low(values), 'head', scatter_dimension=0, tiled=True)  133 us
    all_gather x4, waiting for transfers between devices, gather_rows(): return lax.all_gather(values, 'head', axis=0, tiled=True)  99.6 us
    dot_general x10, matrix products, dot(): lax.dot_general(left, right, (dims, ((), ())), preferred_element_type=F32)  80.5 us
    all_gather x1, waiting for transfers between devices, on_device(): second_set = lax.all_gather(mine, 'dp', axis=0, tiled=True)  73.5 us
    reduce_scatter x1, waiting for transfers between devices, on_device(): lax.psum_scatter(mix_terms, 'dp', scatter_dimension=0, tiled=True)  67.9 us
    all_gather x1, waiting for transfers between devices, on_device(): first_set = lax.all_gather(mine, 'dp', axis=0, tiled=True)  52.4 us
    pallas_call x1, Pallas kernels, mixer_bwd(): pl.pallas_call(mixer_bwd_kernel, grid=(steps,), in_specs=[rows(hg_rows.sh...  45.5 us
    psum x1, blocking collectives, on_device(): lax.psum((attn_gain_grad, mlp_gain_grad, head_gain_grad[0], conv_full), (...  40.5 us
  transfers between devices with their start and end apart: 12, of which 12 were waited for; matrix products, arithmetic and copies ran while one was open for 13% of the time, Pallas kernels for 6%

profile of v1, /device:TPU:0, one launch (start us, length us, event | category | flops | bytes accessed | tf_op | source)
XLA Modules:
  0.0 717.0 jit_solution(11856292105654402870)
XLA Ops:
  21.4 52.4 %all-gather.9.cloned.1.call-done = bf16[1024,1408]{1,0:T(8,128)(2,1)} async-done(((bf16[128,1408]{1,0:T(8,128)(2,1)}), bf16[1024,1408]{1,0:T(8,128)(2,1)}) %all-gather.9.cloned.1.call-update) | async-done | bytes 2883600 | tf_op jit(solution)/shard_map/all_gather | solution.py:426
  73.8 3.3 slice.93.w_ref
  77.1 32.0 %all-gather.7.cloned.1.call-done.x_ref = bf16[2048,1024]{1,0:T(8,128)(2,1)} async-done(((bf16[512,1024]{1,0:T(8,128)(2,1)}), bf16[2048,1024]{1,0:T(8,128)(2,1)}) %all-gather.7.cloned.1.call-update) | async-done | bytes 4194320 | tf_op jit(solution)/shard_map/all_gather | solution.py:398
  109.0 27.6 %mixer_fwd.1 = (f32[2048,1152]{1,0:T(8,128)}, bf16[2048,256]{1,0:T(8,128)(2,1)}, f32[2048,256]{1,0:T(8,128)}, bf16[16,2,128,128]{3,2,1,0:T(8,128)(2,1)}, bf16[16...) custom-call(bf16[2048,1024]{1,0:T(8,128)(2,1)} %all-gather.7.cloned., ...), custom_call_target="tpu_custom_call" | custom-call | tf_op jit(solution)/shard_map/mixer_fwd/pallas_call | solution.py:299
  136.6 4.6 convolution_convert_fusion.5
  143.2 42.7 %reduce-scatter.7.cloned.1.call-done = bf16[512,1024]{1,0:T(8,128)(2,1)} async-done(((bf16[2048,1024]{1,0:T(8,128)(2,1)}), bf16[512,1024]{1,0:T(8,128)(2,1)}) %reduce-scatter.7.cloned.1.call-update) | async-done | bytes 1048592 | tf_op jit(solution)/shard_map/reduce_scatter | solution.py:402
  187.6 2.7 multiply_convert_fusion.1
  191.1 73.5 %all-gather.13.cloned.1.call-done = bf16[1024,2112]{0,1:T(8,128)(2,1)} async-done(((bf16[128,2112]{0,1:T(8,128)(2,1)}), bf16[1024,2112]{0,1:T(8,128)(2,1)}) %all-gather.13.cloned.1.call-update) | async-done | bytes 4325392 | tf_op jit(solution)/shard_map/all_gather | solution.py:428
  264.6 34.2 %all-gather.11.cloned.1.call-done = bf16[2048,1024]{1,0:T(8,128)(2,1)} async-done(((bf16[512,1024]{1,0:T(8,128)(2,1)}), bf16[2048,1024]{1,0:T(8,128)(2,1)}) %all-gather.11.cloned.1.call-update) | async-done | bytes 4194320 | tf_op jit(solution)/shard_map/all_gather | solution.py:398
  298.8 11.7 %fusion.6 = f32[2048,1408]{0,1:T(8,128)} fusion(bf16[2048,1024]{1,0:T(8,128)(2,1)} %all-gather.11.cloned.1.call-done, bf16[1024,2112]{0,1:T(8,128)(2,1)} %all-gather.13.cloned.1.call-done), kind=kOutput, calls=%fused_computation.29 | convolution fusion | flops 5905580032 | bytes 18612224 | tf_op jit(solution)/shard_map/dot_general | solution.py:22
  310.4 24.3 %all-gather.15.cloned.1.call-done = bf16[2048,1024]{1,0:T(8,128)(2,1)} async-done(((bf16[512,1024]{1,0:T(8,128)(2,1)}), bf16[2048,1024]{1,0:T(8,128)(2,1)}) %all-gather.15.cloned.1.call-update) | async-done | bytes 4194320 | tf_op jit(solution)/shard_map/all_gather | solution.py:398
  334.8 11.3 %fusion.2 = (bf16[2048,704]{0,1:T(8,128)(2,1)S(1)}, bf16[2048,704]{0,1:T(8,128)(2,1)S(1)}, bf16[2048,704]{0,1:T(8,128)(2,1)}) fusion(f32[2048,1408]{0,1:T(8,128)} %fusion.6, bf16[2048,1024]{1,0:T(8,128)(2,1)} %all-gather.15.cloned.1.call-done, bf16[1024,2112]{0,1:T(8,128)(2,1)} %all-gather.13.cloned.1.call-done), kind=kOutput, calls=%fused_computation.5 | convolution fusion | flops 2977300480 | bytes 25821184 | tf_op jit(solution)/shard_map/dot_general | solution.py:22
  348.6 8.5 %convolution_convert_fusion.3 = bf16[2048,1024]{1,0:T(8,128)(2,1)} fusion(bf16[2048,704]{0,1:T(8,128)(2,1)S(1)} %get-tuple-element.138, bf16[2048,704]{0,1:T(8,128)(2,1)S(1)} %get-tuple-element.137, bf16[1024,2112]{0,1:T(8,128)(2,1)S(1)} %copy-done.22), kind=kOutput, calls=%fused_computation.20 | convolution fusion | flops 5919211520 | bytes 12845056 | tf_op jit(solution)/shard_map/dot_general | solution.py:22
  357.2 44.6 %reduce-scatter.11.cloned.1.call-done = bf16[512,1024]{1,0:T(8,128)(2,1)} async-done(((bf16[2048,1024]{1,0:T(8,128)(2,1)}), bf16[512,1024]{1,0:T(8,128)(2,1)}) %reduce-scatter.11.cloned.1.call-update) | async-done | bytes 1048592 | tf_op jit(solution)/shard_map/reduce_scatter | solution.py:402
  401.8 2.8 fusion.17
  406.8 7.4 %fusion.25 = bf16[1024,704]{0,1:T(8,128)(2,1)} fusion(bf16[2048,704]{0,1:T(8,128)(2,1)} %get-tuple-element.139, bf16[2048,1024]{1,0:T(8,128)(2,1)} %all-gather.15.cloned.1.call-done), kind=kOutput, calls=%fused_computation.52 | convolution fusion | flops 2953510912 | bytes 8519680 | tf_op jit(solution)/shard_map/dot_general | solution.py:22
  414.1 2.6 copy.116
  416.7 10.4 %convolution_convert_fusion = bf16[1024,1408]{1,0:T(8,128)(2,1)S(1)} fusion(bf16[2048,1024]{1,0:T(8,128)(2,1)} %all-gather.11.cloned.1.call-done, bf16[2048,704]{0,1:T(8,128)(2,1)} %copy-done.25, bf16[2048,704]{0,1:T(8,128)(2,1)} %copy-done.24), kind=kOutput, calls=%fused_computation.17 | convolution fusion | flops 5918556160 | bytes 12845056 | tf_op jit(solution)/shard_map/dot_general | solution.py:22
  427.1 2.4 pad_maximum_fusion.1
  432.0 9.1 %all-gather.17.cloned.1.call-done.hg_ref = bf16[2048,1024]{1,0:T(8,128)(2,1)} async-done(((bf16[512,1024]{1,0:T(8,128)(2,1)}), bf16[2048,1024]{1,0:T(8,128)(2,1)}) %all-gather.17.cloned.1.call-update) | async-done | bytes 4194320 | tf_op jit(solution)/shard_map/all_gather | solution.py:398
  441.1 45.5 %mixer_bwd.1 = (bf16[2048,1152]{1,0:T(8,128)(2,1)}, f32[4,768]{1,0:T(4,128)}, f32[1,128]{1,0:T(1,128)}) custom-call(bf16[2048,1024]{1,0:T(8,128)(2,1)} %all-gather.17.cloned.1.call-done.hg_ref, bf16[1024,256]{1,0:T(8,128)(2,1)} %slice.102.wout_ref, f32[2048,1152]{1,0:T(8,128)} %get-tuple-element.28.pre_ref.halo_ref, ...), custom_call_target="tpu_custom_call" | custom-call | tf_op jit(solution)/shard_map/mixer_bwd/pallas_call | solution.py:334
  486.6 2.7 convolution_convert_fusion.8
  490.7 6.2 convolution_convert_fusion.1
  498.8 10.2 %convolution_convert_fusion.2 = bf16[2048,1024]{1,0:T(8,128)(2,1)} fusion(bf16[2048,1152]{1,0:T(8,128)(2,1)} %get-tuple-element.36, bf16[1024,1408]{1,0:T(8,128)(2,1)} %all-gather.9.cloned.1.call-done), kind=kOutput, calls=%fused_computation.19 | convolution fusion | flops 4833935360 | bytes 11272192 | tf_op jit(solution)/shard_map/dot_general | solution.py:22
  509.0 7.7 %convolution_convert_fusion.4 = bf16[2048,1024]{1,0:T(8,128)(2,1)} fusion(bf16[2048,704]{0,1:T(8,128)(2,1)} %get-tuple-element.139, bf16[1024,2112]{0,1:T(8,128)(2,1)} %all-gather.13.cloned.1.call-done), kind=kOutput, calls=%fused_computation.21 | convolution fusion | flops 2954887168 | bytes 8519680 | tf_op jit(solution)/shard_map/dot_general | solution.py:22
  516.7 19.6 %reduce-scatter.17.cloned.1.call-done = bf16[128,2112]{1,0:T(8,128)(2,1)} async-done(((bf16[1024,2112]{1,0:T(8,128)(2,1)}), bf16[128,2112]{1,0:T(8,128)(2,1)}) %reduce-scatter.17.cloned.1.call-update) | async-done | bytes 540688 | tf_op jit(solution)/shard_map/reduce_scatter | solution.py:462
  543.8 67.9 %reduce-scatter.15.cloned.1.call-done = bf16[128,1408]{1,0:T(8,128)(2,1)} async-done(((bf16[1024,1408]{1,0:T(8,128)(2,1)}), bf16[128,1408]{1,0:T(8,128)(2,1)}) %reduce-scatter.15.cloned.1.call-update) | async-done | bytes 360464 | tf_op jit(solution)/shard_map/reduce_scatter | solution.py:473
  616.7 41.5 %reduce-scatter.13.cloned.1.call-done = bf16[512,1024]{1,0:T(8,128)(2,1)} async-done(((bf16[2048,1024]{1,0:T(8,128)(2,1)}), bf16[512,1024]{1,0:T(8,128)(2,1)}) %reduce-scatter.13.cloned.1.call-update) | async-done | bytes 1048592 | tf_op jit(solution)/shard_map/reduce_scatter | solution.py:402
  658.2 2.1 fusion.24
  660.3 40.5 %all-reduce.5 = (f32[1024]{0:T(1024)}, f32[3,4,1024]{2,1,0:T(4,128)S(1)}, f32[128]{0:T(128)}, f32[1024]{0:T(1024)}) all-reduce(f32[1024]{0:T(1024)S(1)} %get-tuple-element.131, f32[3,4,1024]{2,1,0:T(4,128)S(1)} %constant_dynamic-update-slice_fusion.4, f32[128]{0:T(128)S(1)} %bitcast.74, ...), channel_id=1, replica_groups=mesh['dp'=8,'head'=4] {'dp','head'}, use_global_device_ids=true, to_apply=%region_11.12 | all-reduce | flops 14464 | bytes 115712 | tf_op jit(solution)/shard_map/psum | solution.py:482
  701.4 4.5 reduce-scatter.9.cloned.1.call-done
  705.8 4.1 fusion.12
  (128 shorter events, 42.0 us)
Async XLA Ops:
  7.2 8.2 %copy-start = (bf16[512,1024]{1,0:T(8,128)(2,1)S(1)}, bf16[512,1024]{1,0:T(8,128)(2,1)}, u32[]{:S(2)}) copy-start(bf16[512,1024]{1,0:T(8,128)(2,1)} %param.16) | copy-start | bytes 3145732
  7.2 10.2 %copy-start.23 = (s32[1,8]{1,0:T(1,128)S(1)}, s32[1,8]{1,0:T(1,128)}, u32[]{:S(2)}) copy-start(s32[1,8]{1,0:T(1,128)} %param.17) | copy-start | bytes 100
  7.2 66.6 %all-gather.9.cloned.1.call-start = ((), (), s32[]{:S(2)}) async-start(), calls=%async_computation.7 | async-start | bytes 3244032 | tf_op jit(solution)/shard_map/all_gather | solution.py:426
  13.2 7.5 %copy-start.19 = (bf16[3,4,256]{2,1,0:T(4,128)(2,1)S(1)}, bf16[3,4,256]{2,1,0:T(4,128)(2,1)}, u32[]{:S(2)}) copy-start(bf16[3,4,256]{2,1,0:T(4,128)(2,1)} %param.24) | copy-start | bytes 18436
  13.2 95.8 %all-gather.7.cloned.1.call-start = ((), (), s32[]{:S(2)}) async-start(), calls=%async_computation.6 | async-start | bytes 5242880 | tf_op jit(solution)/shard_map/all_gather | solution.py:398
  17.4 168.5 %reduce-scatter.7.cloned.1.call-start = ((), (), s32[]{:S(2)}) async-start(), calls=%async_computation.8 | async-start | bytes 5242880 | tf_op jit(solution)/shard_map/reduce_scatter | solution.py:402
  141.2 46.3 %copy-start.11 = (f32[1024]{0:T(1024)S(1)}, f32[1024]{0:T(1024)}, u32[]{:S(2)}) copy-start(f32[1024]{0:T(1024)} %param.27) | copy-start | bytes 12292
  141.2 123.3 %all-gather.13.cloned.1.call-start = ((), (), s32[]{:S(2)}) async-start(), calls=%async_computation.10 | async-start | bytes 4866048 | tf_op jit(solution)/shard_map/all_gather | solution.py:428
  143.2 155.6 %all-gather.11.cloned.1.call-start = ((), (), s32[]{:S(2)}) async-start(), calls=%async_computation.9 | async-start | bytes 5242880 | tf_op jit(solution)/shard_map/all_gather | solution.py:398
  187.6 217.0 %copy-start.13 = (f32[512]{0:T(512)}, f32[512]{0:T(512)S(1)}, u32[]{:S(2)}) copy-start(f32[512]{0:T(512)S(1)} %get-tuple-element.164) | copy-start | bytes 6148
  190.3 144.5 %all-gather.15.cloned.1.call-start = ((), (), s32[]{:S(2)}) async-start(), calls=%async_computation.12 | async-start | bytes 5242880 | tf_op jit(solution)/shard_map/all_gather | solution.py:398
  190.9 211.0 %reduce-scatter.11.cloned.1.call-start = ((), (), s32[]{:S(2)}) async-start(), calls=%async_computation.13 | async-start | bytes 5242880 | tf_op jit(solution)/shard_map/reduce_scatter | solution.py:402
  334.8 13.8 %copy-start.22 = (bf16[1024,2112]{0,1:T(8,128)(2,1)S(1)}, bf16[1024,2112]{0,1:T(8,128)(2,1)}, u32[]{:S(2)}) copy-start(bf16[1024,2112]{0,1:T(8,128)(2,1)} %all-gather.13.cloned.1.call-done) | copy-start | bytes 12976132
  346.0 2.5 copy-start.25
  357.1 44.7 %copy-start.1 = (bf16[512,1024]{1,0:T(8,128)(2,1)S(1)}, bf16[512,1024]{1,0:T(8,128)(2,1)}, u32[]{:S(2)}) copy-start(bf16[512,1024]{1,0:T(8,128)(2,1)} %reduce-scatter.7.cloned.1.call-done) | copy-start | bytes 3145732
  357.1 47.5 %copy-start.2 = (bf16[512,1024]{1,0:T(8,128)(2,1)S(1)}, bf16[512,1024]{1,0:T(8,128)(2,1)}, u32[]{:S(2)}) copy-start(bf16[512,1024]{1,0:T(8,128)(2,1)} %param.31) | copy-start | bytes 3145732
  357.1 83.9 %all-gather.17.cloned.1.call-start = ((), (), s32[]{:S(2)}) async-start(), calls=%async_computation.14 | async-start | bytes 5242880 | tf_op jit(solution)/shard_map/all_gather | solution.py:398
  401.8 2.8 copy-start.3
  406.4 129.9 %reduce-scatter.17.cloned.1.call-start = ((), (), s32[]{:S(2)}) async-start(), calls=%async_computation.17 | async-start | bytes 5013504 | tf_op jit(solution)/shard_map/reduce_scatter | solution.py:462
  416.7 10.4 %copy-start.4 = (bf16[1024,704]{1,0:T(8,128)(2,1)S(1)}, bf16[1024,704]{1,0:T(8,128)(2,1)}, u32[]{:S(2)}) copy-start(bf16[1024,704]{1,0:T(8,128)(2,1)} %copy.116) | copy-start | bytes 4325380
  429.6 182.2 %reduce-scatter.15.cloned.1.call-start = ((), (), s32[]{:S(2)}) async-start(), calls=%async_computation.16 | async-start | bytes 3244032 | tf_op jit(solution)/shard_map/reduce_scatter | solution.py:473
  441.1 45.5 %copy-start.5 = (bf16[2048,1024]{1,0:T(8,128)(2,1)S(1)}, bf16[2048,1024]{1,0:T(8,128)(2,1)}, u32[]{:S(2)}) copy-start(bf16[2048,1024]{1,0:T(8,128)(2,1)} %all-gather.17.cloned.1.call-done.hg_ref) | copy-start | bytes 12582916
  486.6 2.7 copy-start.6
  486.6 4.1 copy-start.21
  498.7 159.4 %reduce-scatter.13.cloned.1.call-start = ((), (), s32[]{:S(2)}) async-start(), calls=%async_computation.15 | async-start | bytes 5242880 | tf_op jit(solution)/shard_map/reduce_scatter | solution.py:402
  509.0 196.8 %reduce-scatter.9.cloned.1.call-start = ((), (), s32[]{:S(2)}) async-start(), calls=%async_computation.11 | async-start | bytes 5242880 | tf_op jit(solution)/shard_map/reduce_scatter | solution.py:402
  538.4 119.8 %copy-start.12 = (f32[1024]{0:T(1024)S(1)}, f32[1024]{0:T(1024)}, u32[]{:S(2)}) copy-start(f32[1024]{0:T(1024)} %param.18) | copy-start | bytes 12292
  543.1 117.2 %copy-start.17 = (f32[1024]{0:T(1024)S(1)}, f32[1024]{0:T(1024)}, u32[]{:S(2)}) copy-start(f32[1024]{0:T(1024)} %get-tuple-element.129) | copy-start | bytes 12292
  543.1 117.2 %copy-start.20 = (f32[1,128]{1,0:T(1,128)S(1)}, f32[1,128]{1,0:T(1,128)}, u32[]{:S(2)}) copy-start(f32[1,128]{1,0:T(1,128)} %get-tuple-element.38) | copy-start | bytes 1540
  543.1 162.7 %copy-start.14 = (f32[512]{0:T(512)S(1)}, f32[512]{0:T(512)}, u32[]{:S(2)}) copy-start(f32[512]{0:T(512)} %copy-done.13) | copy-start | bytes 6148
  543.1 162.7 %copy-start.16 = (f32[512]{0:T(512)S(1)}, f32[512]{0:T(512)}, u32[]{:S(2)}) copy-start(f32[512]{0:T(512)} %copy-done.15) | copy-start | bytes 6148
  543.1 162.7 %copy-start.18 = (f32[512]{0:T(512)S(1)}, f32[512]{0:T(512)}, u32[]{:S(2)}) copy-start(f32[512]{0:T(512)} %get-tuple-element.162) | copy-start | bytes 6148
  (6 other events, 7.2 us)
Sparse Core Ops, SparseCore 0:
  13.4 60.3 all-gather.8
  75.9 33.0 all-gather.6
  141.4 44.5 reduce-scatter.6
  188.0 76.4 all-gather.12
  266.0 32.6 all-gather.10
  300.2 34.4 all-gather.14
  357.2 44.5 reduce-scatter.10
  406.6 34.4 all-gather.16
  444.7 91.6 reduce-scatter.16
  540.2 71.5 reduce-scatter.14
  614.5 43.6 reduce-scatter.12
  660.6 45.2 reduce-scatter.8

commit v2 on v1

--- a/solution.py
+++ b/solution.py
@@ -102,7 +102,7 @@
         ext[0:PAD, :] = jnp.zeros((PAD, 3 * hid), F32)
         state[...] = jnp.zeros_like(state)
 
-    pre_ref[...] = dot(x_ref[...], w_ref[...], ((1,), (0,)))
+    pre_ref[...] = dot(x_ref[...], w_ref[:, hid:], ((1,), (0,)))
     aux = aux_ref[...]
     conv = conv_ref[...]
     pre = pre_ref[:, : 3 * hid]
@@ -289,8 +289,8 @@
 
 
 def mixer_fwd(x_rows, weights, aux, docrow, conv, gain):
-    length, width = x_rows.shape[0], weights.shape[1]
     hid = conv.shape[1] // 3
+    length, width = x_rows.shape[0], weights.shape[1] - hid
     heads, chunks = hid // HEAD_DIM, length // CHUNK
     rows = lambda n: pl.BlockSpec((STEP, n), lambda i: (i, 0))
     whole = lambda a: pl.BlockSpec(a.shape, lambda i: (0,) * a.ndim)
@@ -319,7 +319,7 @@
     )(x_rows, weights, aux, docrow, conv, gain)
 
 
-def mixer_bwd(hg_rows, out_t, aux, docrow, conv, gain, saved):
+def mixer_bwd(hg_rows, weights, aux, docrow, conv, gain, saved):
     pre, o, t, phi, s, p, d, ew = saved
     length, width = pre.shape
     hid = conv.shape[1] // 3
@@ -335,7 +335,7 @@
         mixer_bwd_kernel,
         grid=(steps,),
         in_specs=[
-            rows(hg_rows.shape[1]), whole(out_t), rows(width), halo, rows(aux.shape[1]),
+            rows(hg_rows.shape[1]), pl.BlockSpec((weights.shape[0], hid), lambda i: (0, 0)), rows(width), halo, rows(aux.shape[1]),
             pl.BlockSpec((1, GROUP, CHUNK), lambda i: (last - i, 0, 0)), whole(conv), whole(gain),
             rows(hid),
         ]
@@ -357,7 +357,486 @@
         ],
         compiler_params=pltpu.CompilerParams(vmem_limit_bytes=VMEM_LIMIT),
         name="mixer_bwd",
-    )(hg_rows, out_t, pre, pre, aux, docrow, conv, gain, o, t, phi, s, p, d, ew)
+    )(hg_rows, weights, pre, pre, aux, docrow, conv, gain, o, t, phi, s, p, d, ew)
+
+
+MESH = pl.DeviceIdType.MESH
+
+
+def remote(src, dst, sent, landed, axis, to):
+    return pltpu.make_async_remote_copy(
+        src_ref=src, dst_ref=dst, send_sem=sent, recv_sem=landed,
+        device_id={axis: to}, device_id_type=MESH,
+    )
+
+
+def shard_line(lines, own, out, sems):
+    right_s, left_s, over_s, landed, local = sems
+    me = lax.axis_index("dp")
+    spot, side = me // 2, me % 2
+    slot = lambda place: 2 * place + side
+    across = me + 1 - 2 * side
+
+    def hop(step, where):
+        return (spot - step, me + 2, right_s) if where == 0 else (spot + step, me - 2, left_s)
+
+    def going(step, where):
+        place, to, sent = hop(step, where)
+        src = out.at[slot(place)] if not isinstance(step, int) or step else own
+        return remote(src, out.at[slot(place)], sent.at[step], landed.at[slot(place)], "dp", to)
+
+    def goes(step, where):
+        if where == 0:
+            return jnp.logical_and(spot - step >= 0, spot + 1 < lines)
+        return jnp.logical_and(spot + step < lines, spot >= 1)
+
+    def over(place):
+        return remote(out.at[slot(place)], out.at[slot(place)], over_s.at[place], landed.at[slot(place)], "dp", across)
+
+    def first():
+        pltpu.make_async_copy(own, out.at[me], local).start()
+        remote(own, out.at[me], over_s.at[spot], landed.at[me], "dp", across).start()
+        for where in (0, 1):
+            pl.when(goes(0, where))(lambda where=where: going(0, where).start())
+
+    def arrive(step, place):
+        @pl.when(jnp.logical_and(place >= 0, place < lines))
+        def _():
+            over(place).wait_recv()
+            over(place).start()
+
+    def hop_step(step):
+        for where in (0, 1):
+            place = spot - step - 1 if where == 0 else spot + step + 1
+            arrive(step, place)
+            if isinstance(step, int) and step + 1 >= lines - 1:
+                continue
+            pl.when(jnp.logical_and(goes(step + 1, where), step + 1 < lines - 1))(
+                lambda where=where: going(step + 1, where).start()
+            )
+
+    def last():
+        pltpu.make_async_copy(own, out.at[me], local).wait()
+
+        @pl.loop(0, lines)
+        def _(place):
+            there = 2 * place + 1 - side
+            remote(out.at[there], out.at[there], over_s.at[place], landed.at[there], "dp", across).wait_recv()
+            over(place).wait_send()
+
+        @pl.loop(0, lines - 1)
+        def _(step):
+            for where in (0, 1):
+                pl.when(goes(step, where))(lambda where=where: going(step, where).wait_send())
+
+    return first, hop_step, last
+
+
+def greet(lines, count):
+    barrier = pltpu.get_barrier_semaphore()
+    me = lax.axis_index("dp")
+    spot, across = me // 2, me + 1 - 2 * (me % 2)
+
+    def tell(axis, to):
+        pl.semaphore_signal(barrier, 1, device_id={axis: to}, device_id_type=MESH)
+
+    tell("dp", across)
+    pl.when(spot >= 1)(lambda: tell("dp", me - 2))
+    pl.when(spot + 1 < lines)(lambda: tell("dp", me + 2))
+    head = lax.axis_index("head")
+    tell("head", head + 1 - 2 * (head % 2))
+    for f in range(1, count // 2):
+        tell("head", lax.rem(head + 2 * f, count))
+    beside = jnp.minimum(spot, 1) + jnp.minimum(lines - 1 - spot, 1)
+    pl.semaphore_wait(barrier, 1 + count // 2 + beside)
+
+
+def start_kernel(lines, count, parts, tok_ref, gain_ref, w_ref, rows_ref, wall_ref, mine,
+                 right_s, left_s, over_s, landed, local, far_s, pair_s, fwd_s, got, keep_s):
+    greet(lines, count)
+    first, hop_step, last = shard_line(lines, w_ref, wall_ref, (right_s, left_s, over_s, landed, local.at[0]))
+    first()
+    me = lax.axis_index("head")
+    pair = me + 1 - 2 * (me % 2)
+    fars = [lax.rem(me + 2 * f, count) for f in range(1, count // 2)]
+    size = tok_ref.shape[0] // parts
+    span = lambda p: pl.ds(p * size, size)
+
+    def block(owner, p):
+        return rows_ref.at[owner, span(p)]
+
+    for p in range(parts):
+        x = tok_ref[p * size : (p + 1) * size, :].astype(F32)
+        inv = lax.rsqrt(jnp.mean(x * x, axis=-1, keepdims=True) + 1e-6)
+        mine[p * size : (p + 1) * size, :] = (x * inv * gain_ref[...]).astype(BF16)
+        for f, far in enumerate(fars):
+            remote(mine.at[span(p)], block(me, p), far_s.at[f, p], got.at[me, p], "head", far).start()
+        remote(mine.at[span(p)], block(me, p), pair_s.at[p], got.at[me, p], "head", pair).start()
+        pltpu.make_async_copy(mine.at[span(p)], block(me, p), keep_s.at[p]).start()
+
+    def pass_on(p):
+        for f, far in enumerate(fars):
+            moved = remote(block(far, p), block(far, p), fwd_s.at[f, p], got.at[far, p], "head", pair)
+            moved.wait_recv()
+            moved.start()
+
+    for i in range(parts):
+        pass_on(i)
+        if i < lines - 1:
+            hop_step(i)
+    if lines - 1 > parts:
+        pl.loop(parts, lines - 1)(hop_step)
+    last()
+    for p in range(parts):
+        remote(mine.at[span(p)], block(pair, p), pair_s.at[p], got.at[pair, p], "head", pair).wait()
+        pltpu.make_async_copy(mine.at[span(p)], block(me, p), keep_s.at[p]).wait()
+        for f, far in enumerate(fars):
+            remote(mine.at[span(p)], block(me, p), far_s.at[f, p], got.at[me, p], "head", far).wait_send()
+            there = lax.rem(pair + 2 * (f + 1), count)
+            remote(block(far, p), block(there, p), fwd_s.at[f, p], got.at[there, p], "head", pair).wait()
+
+
+def start(tokens, gain, mine, n_dp, n_head, parts=4):
+    rows, width = tokens.shape
+    lines, far = n_dp // 2, n_head // 2 - 1
+    dma = lambda *shape: pltpu.SemaphoreType.DMA(shape)
+    anywhere = pl.BlockSpec(memory_space=pl.ANY)
+    vmem = pl.BlockSpec(memory_space=pltpu.VMEM)
+    return pl.pallas_call(
+        partial(start_kernel, lines, n_head, parts),
+        out_shape=[jax.ShapeDtypeStruct((n_head, rows, width), BF16),
+                   jax.ShapeDtypeStruct((n_dp, *mine.shape), BF16)],
+        in_specs=[vmem, vmem, anywhere],
+        out_specs=[anywhere, anywhere],
+        scratch_shapes=[
+            pltpu.VMEM((rows, width), BF16),
+            dma(lines), dma(lines), dma(lines), dma(n_dp), dma(1),
+            dma(far, parts), dma(parts), dma(far, parts), dma(n_head, parts), dma(parts),
+        ],
+        compiler_params=pltpu.CompilerParams(vmem_limit_bytes=VMEM_LIMIT, has_side_effects=True, collective_id=0),
+        name="start",
+    )(tokens, gain, mine)
+
+
+class HeadScatter:
+    def __init__(self, count, parts, refs):
+        self.count, self.parts = count, parts
+        (self.out, self.near, self.onward, self.far, self.own,
+         self.out_s, self.near_r, self.onward_s, self.far_r) = refs
+        self.me = lax.axis_index("head")
+        self.side, self.place = self.me % 2, self.me // 2
+        self.pair = self.me + 1 - 2 * self.side
+        self.size = self.own.shape[0] // parts
+
+    @staticmethod
+    def scratch(count, parts, rows, width):
+        size, half = rows // parts, count // 2
+        return [
+            pltpu.VMEM((2, 2, half, size, width), BF16),
+            pltpu.VMEM((parts, half, size, width), BF16),
+            pltpu.VMEM((2, half - 1, size, width), BF16),
+            pltpu.VMEM((parts, half - 1, size, width), BF16),
+            pltpu.VMEM((rows, width), F32),
+            pltpu.SemaphoreType.DMA((2,)),
+            pltpu.SemaphoreType.DMA((parts,)),
+            pltpu.SemaphoreType.DMA((2, half - 1)),
+            pltpu.SemaphoreType.DMA((parts, half - 1)),
+        ]
+
+    def _near(self, p):
+        slot = p % 2
+        return remote(self.out.at[slot, 1 - self.side], self.near.at[p], self.out_s.at[slot], self.near_r.at[p], "head", self.pair)
+
+    def _far(self, p, f):
+        slot = p % 2
+        to = lax.rem(self.me + 2 * (f + 1), self.count)
+        return remote(self.onward.at[slot, f], self.far.at[p, f], self.onward_s.at[slot, f], self.far_r.at[p, f], "head", to)
+
+    def offer(self, p, total):
+        if p >= 2:
+            self._near(p - 2).wait_send()
+        for owner in range(self.count):
+            self.out[p % 2, owner % 2, owner // 2] = total[owner * self.size : (owner + 1) * self.size].astype(BF16)
+        self._near(p).start()
+
+    def turn(self, p):
+        slot, half = p % 2, self.count // 2
+        self._near(p).wait_recv()
+        both = lambda i: self.out[slot, self.side, i].astype(F32) + self.near[p, i].astype(F32)
+        for f in range(half - 1):
+            if p >= 2:
+                self._far(p - 2, f).wait_send()
+            self.onward[slot, f] = both(lax.rem(self.place + f + 1, half)).astype(BF16)
+            self._far(p, f).start()
+        self.own[p * self.size : (p + 1) * self.size, :] = both(self.place)
+
+    def take(self, p):
+        total = self.own[p * self.size : (p + 1) * self.size, :]
+        for f in range(self.count // 2 - 1):
+            self._far(p, f).wait_recv()
+            total = total + self.far[p, f].astype(F32)
+        return total
+
+    def close(self):
+        for p in range(max(self.parts - 2, 0), self.parts):
+            self._near(p).wait_send()
+            for f in range(self.count // 2 - 1):
+                self._far(p, f).wait_send()
+
+
+class DpScatter:
+    def __init__(self, lines, terms, refs):
+        self.lines, self.terms = lines, terms
+        self.cross, self.going, self.coming, self.cross_s, self.cross_r, self.go_s, self.come_r = refs
+        self.me = lax.axis_index("dp")
+        self.spot, self.side = self.me // 2, self.me % 2
+        self.across = self.me + 1 - 2 * self.side
+
+    @staticmethod
+    def scratch(lines, rows, width):
+        return [
+            pltpu.VMEM((lines, rows, width), BF16),
+            pltpu.VMEM((2, lines, rows, width), BF16),
+            pltpu.VMEM((2, lines, rows, width), BF16),
+            pltpu.SemaphoreType.DMA((lines,)),
+            pltpu.SemaphoreType.DMA((lines,)),
+            pltpu.SemaphoreType.DMA((2, lines)),
+            pltpu.SemaphoreType.DMA((2, lines)),
+        ]
+
+    def _cross(self, place):
+        return remote(self.terms.at[2 * place + 1 - self.side], self.cross.at[place], self.cross_s.at[place], self.cross_r.at[place], "dp", self.across)
+
+    def _line(self, way, dest):
+        to = self.me + 2 if way == 0 else self.me - 2
+        return remote(self.going.at[way, dest], self.coming.at[way, dest], self.go_s.at[way, dest], self.come_r.at[way, dest], "dp", to)
+
+    def offer(self, place):
+        self._cross(place).start()
+
+    def _both(self, place):
+        return self.terms[2 * place + self.side].astype(F32) + self.cross[place].astype(F32)
+
+    def _passes(self, way, dest):
+        return dest > self.spot if way == 0 else dest < self.spot
+
+    def _fed(self, way):
+        return self.spot >= 1 if way == 0 else self.spot + 1 < self.lines
+
+    def step(self, d):
+        for way in (0, 1):
+            dest = self.lines - 1 - d if way == 0 else d
+
+            @pl.when(self._passes(way, dest))
+            def _(way=way, dest=dest):
+                self._cross(dest).wait_recv()
+                self.going[way, dest] = self._both(dest).astype(BF16)
+
+                @pl.when(self._fed(way))
+                def _():
+                    self._line(way, dest).wait_recv()
+                    self.going[way, dest] = (
+                        self.going[way, dest].astype(F32) + self.coming[way, dest].astype(F32)
+                    ).astype(BF16)
+
+                self._line(way, dest).start()
+
+    def finish(self, out_ref):
+        self._cross(self.spot).wait_recv()
+        out_ref[...] = self._both(self.spot)
+        for way in (0, 1):
+            @pl.when(self._fed(way))
+            def _(way=way):
+                self._line(way, self.spot).wait_recv()
+                out_ref[...] += self.coming[way, self.spot].astype(F32)
+
+    def close(self):
+        @pl.loop(0, self.lines)
+        def _(place):
+            self._cross(place).wait_send()
+            for way in (0, 1):
+                pl.when(self._passes(way, place))(lambda way=way: self._line(way, place).wait_send())
+
+
+class SmallSum:
+    def __init__(self, n_dp, count, shared, refs):
+        self.n_dp, self.count, self.shared = n_dp, count, shared
+        self.mine, self.theirs, self.half, self.halves, self.a_s, self.a_r, self.b_s, self.b_r = refs
+        self.dp, self.head = lax.axis_index("dp"), lax.axis_index("head")
+
+    @staticmethod
+    def scratch(n_dp, count, rows, shared):
+        return [
+            pltpu.VMEM((rows, 128), F32),
+            pltpu.VMEM((n_dp, rows, 128), F32),
+            pltpu.VMEM((shared, 128), F32),
+            pltpu.VMEM((count, shared, 128), F32),
+            pltpu.SemaphoreType.DMA((n_dp,)),
+            pltpu.SemaphoreType.DMA((n_dp,)),
+            pltpu.SemaphoreType.DMA((count,)),
+            pltpu.SemaphoreType.DMA((count,)),
+        ]
+
+    def _a(self, hop):
+        to = lax.rem(self.dp + hop, self.n_dp)
+        return remote(self.mine, self.theirs.at[self.dp], self.a_s.at[hop], self.a_r.at[self.dp], "dp", to)
+
+    def _b(self, hop):
+        to = lax.rem(self.head + hop, self.count)
+        return remote(self.half, self.halves.at[self.head], self.b_s.at[hop], self.b_r.at[self.head], "head", to)
+
+    def run(self, out_ref):
+        self.theirs[self.dp] = self.mine[...]
+
+        @pl.loop(1, self.n_dp)
+        def _(hop):
+            self._a(hop).start()
+
+        @pl.loop(1, self.n_dp)
+        def _(hop):
+            sender = lax.rem(self.dp + self.n_dp - hop, self.n_dp)
+            remote(self.mine, self.theirs.at[sender], self.a_s.at[hop], self.a_r.at[sender], "dp", sender).wait_recv()
+
+        total = self.theirs[0]
+        for i in range(1, self.n_dp):
+            total = total + self.theirs[i]
+        out_ref[...] = total
+        self.half[...] = total[: self.shared]
+        self.halves[self.head] = total[: self.shared]
+        for hop in range(1, self.count):
+            self._b(hop).start()
+        for hop in range(1, self.count):
+            sender = lax.rem(self.head + self.count - hop, self.count)
+            remote(self.half, self.halves.at[sender], self.b_s.at[hop], self.b_r.at[sender], "head", sender).wait_recv()
+        total = self.halves[0]
+        for i in range(1, self.count):
+            total = total + self.halves[i]
+        out_ref[: self.shared, :] = total
+
+        @pl.loop(1, self.n_dp)
+        def _(hop):
+            self._a(hop).wait_send()
+
+        for hop in range(1, self.count):
+            self._b(hop).wait_send()
+
+
+def greet_all(n_dp, count):
+    barrier = pltpu.get_barrier_semaphore()
+    dp, head = lax.axis_index("dp"), lax.axis_index("head")
+
+    @pl.loop(1, n_dp)
+    def _(hop):
+        pl.semaphore_signal(barrier, 1, device_id={"dp": lax.rem(dp + hop, n_dp)}, device_id_type=MESH)
+
+    for hop in range(1, count):
+        pl.semaphore_signal(barrier, 1, device_id={"head": lax.rem(head + hop, count)}, device_id_type=MESH)
+    pl.semaphore_wait(barrier, n_dp + count - 2)
+
+
+def end_kernel(n_dp, count, parts, shared,
+               dpre_ref, w_ref, normed_ref, hg_ref, mixed_ref, tok_ref, gain_ref, grad_ref, small_ref,
+               in_ref, mix_ref, sum_ref, *scratch):
+    scratch = list(scratch)
+    take = lambda n: [scratch.pop(0) for _ in range(n)]
+    head_refs, dp_refs, small_refs = take(9), take(7), take(8)
+    terms, dpre, w, normed, hg, mixed, loads = scratch
+    rows, width = tok_ref.shape
+    block = terms.shape[1]
+    hid = mixed.shape[1]
+    greet_all(n_dp, count)
+    moves = [pltpu.make_async_copy(s, d, loads.at[i]) for i, (s, d) in enumerate(
+        ((dpre_ref, dpre), (w_ref.at[:, hid:], w), (normed_ref, normed), (mixed_ref, mixed), (hg_ref, hg)))]
+    for m in moves:
+        m.start()
+    heads = HeadScatter(count, parts, head_refs)
+    line = DpScatter(n_dp // 2, terms, dp_refs)
+    small = SmallSum(n_dp, count, shared, small_refs)
+    size = rows // parts
+
+    def offer(p):
+        part = jnp.concatenate([dpre[o * rows + p * size : o * rows + (p + 1) * size, :] for o in range(count)], axis=0)
+        heads.offer(p, dot(part, w[...], ((1,), (1,))))
+
+    tiles = width // 256
+    per = 256 // block
+
+    def outer(t):
+        cols = slice(t * 256, (t + 1) * 256)
+        left = dot(normed[:, cols], dpre[...], ((0,), (0,))).astype(BF16)
+        right = dot(hg[:, cols], mixed[...], ((0,), (0,))).astype(BF16)
+        for b in range(per):
+            terms[t * per + b, :, :hid] = right[b * block : (b + 1) * block]
+            terms[t * per + b, :, hid:] = left[b * block : (b + 1) * block]
+        for place in range(t * per // 2, (t + 1) * per // 2):
+            line.offer(place)
+
+    order = [t // 2 if t % 2 else tiles - 1 - t // 2 for t in range(tiles)]
+    moves[0].wait()
+    moves[1].wait()
+    offer(0)
+    for m in moves[2:]:
+        m.wait()
+    for i in range(max(tiles, parts)):
+        if i < tiles:
+            outer(order[i])
+        if i < parts:
+            heads.turn(i)
+        if i + 1 < parts:
+            offer(i + 1)
+    small.mine[...] = small_ref[...]
+    gain_total = jnp.zeros((1, width), F32)
+    gain = gain_ref[...]
+
+    def finish(p):
+        at = slice(p * size, (p + 1) * size)
+        normed_grad = heads.take(p).astype(BF16).astype(F32)
+        x = tok_ref[at, :].astype(F32)
+        inv = lax.rsqrt(jnp.mean(x * x, axis=-1, keepdims=True) + 1e-6)
+        scaled = normed_grad * gain
+        mean = jnp.mean(scaled * x, axis=-1, keepdims=True)
+        in_ref[at, :] = grad_ref[at, :] + inv * scaled - x * (inv * inv * inv * mean)
+        return jnp.sum(normed_grad * x * inv, axis=0, keepdims=True)
+
+    lines = n_dp // 2
+    for i in range(parts):
+        gain_total = gain_total + finish(i)
+        if i < lines - 1:
+            line.step(i)
+    if lines - 1 > parts:
+        pl.loop(parts, lines - 1)(line.step)
+    for i in range(width // 128):
+        small.mine[i : i + 1, :] = gain_total[:, i * 128 : (i + 1) * 128]
+    line.finish(mix_ref)
+    small.run(sum_ref)
+    heads.close()
+    line.close()
+
+
+def end(dpre, weights, normed_rows, hg_rows, mixed, tokens, gain, hidden_grad, small, n_dp, count, shared, parts=4):
+    rows, width = tokens.shape
+    block = width // n_dp
+    wide = weights.shape[1]
+    anywhere = pl.BlockSpec(memory_space=pl.ANY)
+    vmem = pl.BlockSpec(memory_space=pltpu.VMEM)
+    like = lambda a: pltpu.VMEM(a.shape, a.dtype)
+    return pl.pallas_call(
+        partial(end_kernel, n_dp, count, parts, shared),
+        out_shape=[
+            jax.ShapeDtypeStruct((rows, width), F32),
+            jax.ShapeDtypeStruct((block, wide), F32),
+            jax.ShapeDtypeStruct(small.shape, F32),
+        ],
+        in_specs=[anywhere] * 5 + [vmem] * 4,
+        out_specs=[vmem] * 3,
+        scratch_shapes=HeadScatter.scratch(count, parts, rows, width)
+        + DpScatter.scratch(n_dp // 2, block, wide)
+        + SmallSum.scratch(n_dp, count, small.shape[0], shared)
+        + [pltpu.VMEM((n_dp, block, wide), BF16), like(dpre), pltpu.VMEM((width, dpre.shape[1]), BF16), like(normed_rows), like(hg_rows), like(mixed),
+           pltpu.SemaphoreType.DMA((5,))],
+        compiler_params=pltpu.CompilerParams(vmem_limit_bytes=VMEM_LIMIT, has_side_effects=True, collective_id=1),
+        name="end",
+    )(dpre, weights, normed_rows, hg_rows, mixed, tokens, gain, hidden_grad, small)
 
 
 def doc_tables(lengths, length):
@@ -422,22 +901,22 @@
 ):
     hid, heads, ff = w_query.shape[1], w_beta.shape[1], w_mlp_gate.shape[1]
     beta_wide = jnp.pad(w_beta, ((0, 0), (0, HEAD_DIM - heads)))
-    mine = jnp.concatenate([w_query, w_key, w_value, w_gate_out, beta_wide, w_out.T], axis=1)
-    first_set = lax.all_gather(mine, "dp", axis=0, tiled=True)
+    mine = jnp.concatenate([w_out.T, w_query, w_key, w_value, w_gate_out, beta_wide], axis=1)
+    n_dp, n_head = lax.axis_size("dp"), lax.axis_size("head")
+    normed_rows, first_set = start(tokens, attn_gain[None, :], mine, n_dp, n_head)
+    normed_rows = normed_rows.reshape(-1, normed_rows.shape[2])
+    first_set = first_set.reshape(-1, first_set.shape[2])
     mine = jnp.concatenate([w_mlp_gate, w_mlp_up, w_down.T], axis=1)
     second_set = lax.all_gather(mine, "dp", axis=0, tiled=True)
-    mix_width = 4 * hid + HEAD_DIM
-    w_mix, out_t = first_set[:, :mix_width], first_set[:, mix_width:]
+    out_t = first_set[:, :hid]
     w_ff, down_t = second_set[:, : 2 * ff], second_set[:, 2 * ff :]
 
     x = tokens.astype(F32)
-    x_inv = inverse_rms(x)
-    normed_rows = gather_rows(low(x * x_inv * attn_gain))
     length = normed_rows.shape[0]
     aux, docrow = doc_tables(lengths[0], length)
     conv = jnp.swapaxes(conv_weight.astype(F32), 0, 1).reshape(conv_weight.shape[1], 3 * hid)
     gain = head_gain[None, :]
-    pre, mixed, *saved = mixer_fwd(normed_rows, w_mix, aux, docrow, conv, gain)
+    pre, mixed, *saved = mixer_fwd(normed_rows, first_set, aux, docrow, conv, gain)
     attention = scatter_rows(dot(mixed, out_t, ((1,), (1,))))
     hidden = x + attention
     h_inv = inverse_rms(hidden)
@@ -464,37 +943,38 @@
     hidden_grad = cotangent.astype(F32) + from_mlp
     hg_rows = gather_rows(low(hidden_grad))
     dpre, conv_part, head_gain_grad = mixer_bwd(
-        hg_rows, out_t, aux, docrow, conv, gain, (pre, *saved)
+        hg_rows, first_set, aux, docrow, conv, gain, (pre, *saved)
     )
-    normed_grad = low(scatter_rows(dot(dpre, w_mix, ((1,), (1,))))).astype(F32)
-    mix_terms = jnp.concatenate(
-        [low(outer(normed_rows, dpre)), low(outer(hg_rows, mixed))], axis=1
+    taps = conv_part.shape[0]
+    shared = 2 * (x.shape[1] // 128) + 8
+    small = jnp.concatenate(
+        [
+            jnp.zeros((x.shape[1] // 128, 128), F32),
+            mlp_gain_grad.reshape(-1, 128),
+            jnp.pad(head_gain_grad, ((0, 7), (0, 0))),
+            conv_part.reshape(-1, 128),
+        ]
     )
-    mix_reduced = lax.psum_scatter(mix_terms, "dp", scatter_dimension=0, tiled=True).astype(F32)
-    from_mixer, attn_gain_grad = norm_back(normed_grad, x, x_inv, attn_gain)
-    input_grad = hidden_grad + from_mixer
-
-    taps = conv_part.shape[0]
-    conv_local = jnp.swapaxes(conv_part.reshape(taps, 3, hid), 0, 1)
-    start = lax.axis_index("head") * hid
-    conv_full = jnp.zeros((3, taps, hid * lax.axis_size("head")), F32)
-    conv_full = lax.dynamic_update_slice(conv_full, conv_local, (0, 0, start))
-    summed = lax.psum((attn_gain_grad, mlp_gain_grad, head_gain_grad[0], conv_full), ("dp", "head"))
-    conv_grad = lax.dynamic_slice_in_dim(summed[3], start, hid, 2)
-    part = lambda i: mix_reduced[:, i * hid : (i + 1) * hid]
+    input_grad, mix_reduced, summed = end(
+        dpre, first_set, normed_rows, hg_rows, mixed, tokens, attn_gain[None, :], hidden_grad, small,
+        n_dp, n_head, shared,
+    )
+    gains = summed[: shared - 8].reshape(2, -1)
+    conv_grad = jnp.swapaxes(summed[shared:].reshape(taps, 3, hid), 0, 1)
+    part = lambda i: mix_reduced[:, (i + 1) * hid : (i + 2) * hid]
     return (
         output,
         input_grad,
-        summed[0],
+        gains[0],
         part(0),
         part(1),
         part(2),
-        mix_reduced[:, 4 * hid : 4 * hid + heads],
+        mix_reduced[:, 5 * hid : 5 * hid + heads],
         part(3),
         conv_grad,
-        summed[2],
-        mix_reduced[:, mix_width:].T,
-        summed[1],
+        summed[shared - 8],
+        mix_reduced[:, :hid].T,
+        gains[1],
         mlp_reduced[:, :ff],
         mlp_reduced[:, ff : 2 * ff],
         mlp_reduced[:, 2 * ff :].T,

time: 725 us -> 602 us (0.83)
  waiting for transfers between devices: 447 us -> 268 us
  Pallas kernels: 73.1 us -> 188 us
  blocking collectives: 40.5 us -> 0 us
  matrix products: 80.5 us -> 61.5 us
  starting transfers between devices: 1.42 us -> 12.7 us
  other arithmetic: 28 us -> 19.7 us
    pallas_call x0 -> x2, Pallas kernels: none -> 115 us  [the longest x1 73.8 us: end(): pl.pallas_call(partial(end_kernel, n_dp, count, parts, shared), out_shape...]
    reduce_scatter x1, waiting for transfers between devices: 19.6 us -> 91 us  [on_device(): lax.psum_scatter(mlp_terms, 'dp', scatter_dimension=0, tiled=True)]
    reduce_scatter x1 -> x0, waiting for transfers between devices: 67.9 us -> none  [on_device(): lax.psum_scatter(mix_terms, 'dp', scatter_dimension=0, tiled=True)]
    all_gather x1 -> x0, waiting for transfers between devices: 52.4 us -> none  [on_device(): first_set = lax.all_gather(mine, 'dp', axis=0, tiled=True)]
    reduce_scatter x4 -> x3, waiting for transfers between devices: 133 us -> 88.8 us  [scatter_rows(): lax.psum_scatter(low(values), 'head', scatter_dimension=0, tiled=True)]
    all_gather x1, waiting for transfers between devices: 73.5 us -> 29.2 us  [on_device(): second_set = lax.all_gather(mine, 'dp', axis=0, tiled=True)]
    all_gather x4 -> x3, waiting for transfers between devices: 99.6 us -> 58.8 us  [gather_rows(): return lax.all_gather(values, 'head', axis=0, tiled=True)]
    psum x1 -> x0, blocking collectives: 40.5 us -> none  [on_device(): lax.psum((attn_gain_grad, mlp_gain_grad, head_gain_grad[0], conv_full), (...]
  transfers between devices with their start and end apart: 12 -> 8, of which waited for: 12 -> 7; matrix products, arithmetic and copies ran while one was open for 13% -> 10% of each run, Pallas kernels for 6% -> 0%
where the time goes in v2:
time: 602 us; the launch traced here: 594 us
  waiting for transfers between devices  268 us (45%)
  Pallas kernels  188 us (31%)
  matrix products  61.5 us (10%)
  local copies, waits for them, and re-layouts  28 us (5%)
  other arithmetic  19.7 us (3%)
  between operations  16.1 us (3%)
  starting transfers between devices  12.7 us (2%)
    reduce_scatter x1, waiting for transfers between devices, on_device(): lax.psum_scatter(mlp_terms, 'dp', scatter_dimension=0, tiled=True)  91 us
    reduce_scatter x3, waiting for transfers between devices, scatter_rows(): lax.psum_scatter(low(values), 'head', scatter_dimension=0, tiled=True)  88.8 us
    pallas_call x1, Pallas kernels, end(): pl.pallas_call(partial(end_kernel, n_dp, count, parts, shared), out_shape...  73.8 us
    dot_general x7, matrix products, dot(): lax.dot_general(left, right, (dims, ((), ())), preferred_element_type=F32)  61.5 us
    all_gather x3, waiting for transfers between devices, gather_rows(): return lax.all_gather(values, 'head', axis=0, tiled=True)  58.8 us
    pallas_call x1, Pallas kernels, mixer_bwd(): pl.pallas_call(mixer_bwd_kernel, grid=(steps,), in_specs=[rows(hg_rows.sh...  45.4 us
    pallas_call x1, Pallas kernels, start(): pl.pallas_call(partial(start_kernel, lines, n_head, parts), out_shape=[ja...  41.1 us
    all_gather x1, waiting for transfers between devices, on_device(): second_set = lax.all_gather(mine, 'dp', axis=0, tiled=True)  29.2 us
  transfers between devices with their start and end apart: 8, of which 7 were waited for; matrix products, arithmetic and copies ran while one was open for 10% of the time, Pallas kernels for 0%

profile of v2, /device:TPU:0, one launch (start us, length us, event | category | flops | bytes accessed | tf_op | source)
XLA Modules:
  0.0 594.4 jit_solution(10834733865167427024)
XLA Ops:
  10.6 1.4 copy.112.aux_ref
  13.7 1.3 reshape.206
  19.2 41.1 %start.1 = (bf16[4,512,1024]{2,1,0:T(8,128)(2,1)}, bf16[8,128,1408]{2,1,0:T(8,128)(2,1)}) custom-call(bf16[512,1024]{1,0:T(8,128)(2,1)} %tok_ref.3, f32[1,1024]{1,0:T(1,128)} %bitcast.80, bf16[128,1408]{1,0:T(8,128)(2,1)} %copy-done.4), custom_call_target="tpu_custom_call" | custom-call | tf_op jit(solution)/shard_map/start/pallas_call | solution.py:505
  60.3 27.7 %mixer_fwd.1 = (f32[2048,1152]{1,0:T(8,128)}, bf16[2048,256]{1,0:T(8,128)(2,1)}, f32[2048,256]{1,0:T(8,128)}, bf16[16,2,128,128]{3,2,1,0:T(8,128)(2,1)}, bf16[16...) custom-call(bf16[2048,1024]{1,0:T(8,128)(2,1)} %bitcast.60, ...), custom_call_target="tpu_custom_call" | custom-call | tf_op jit(solution)/shard_map/mixer_fwd/pallas_call | solution.py:299
  88.0 4.6 convolution_convert_fusion.3
  94.6 40.9 %reduce-scatter.5.cloned.1.call-done = bf16[512,1024]{1,0:T(8,128)(2,1)} async-done(((bf16[2048,1024]{1,0:T(8,128)(2,1)}), bf16[512,1024]{1,0:T(8,128)(2,1)}) %reduce-scatter.5.cloned.1.call-update) | async-done | bytes 1048592 | tf_op jit(solution)/shard_map/reduce_scatter | solution.py:881
  135.5 1.6 multiply_reduce_fusion
  137.2 2.6 multiply_convert_fusion.1
  140.7 29.2 %all-gather.7.cloned.1.call-done = bf16[1024,2112]{0,1:T(8,128)(2,1)} async-done(((bf16[128,2112]{0,1:T(8,128)(2,1)}), bf16[1024,2112]{0,1:T(8,128)(2,1)}) %all-gather.7.cloned.1.call-update) | async-done | bytes 4325392 | tf_op jit(solution)/shard_map/all_gather | solution.py:910
  169.8 34.6 %all-gather.5.cloned.1.call-done = bf16[2048,1024]{1,0:T(8,128)(2,1)} async-done(((bf16[512,1024]{1,0:T(8,128)(2,1)}), bf16[2048,1024]{1,0:T(8,128)(2,1)}) %all-gather.5.cloned.1.call-update) | async-done | bytes 4194320 | tf_op jit(solution)/shard_map/all_gather | solution.py:877
  204.5 11.7 %fusion.6 = f32[2048,1408]{0,1:T(8,128)} fusion(bf16[2048,1024]{1,0:T(8,128)(2,1)} %all-gather.5.cloned.1.call-done, bf16[1024,2112]{0,1:T(8,128)(2,1)} %all-gather.7.cloned.1.call-done), kind=kOutput, calls=%fused_computation.19 | convolution fusion | flops 5905580032 | bytes 18612224 | tf_op jit(solution)/shard_map/dot_general | solution.py:22
  216.1 24.2 %all-gather.9.cloned.1.call-done = bf16[2048,1024]{1,0:T(8,128)(2,1)} async-done(((bf16[512,1024]{1,0:T(8,128)(2,1)}), bf16[2048,1024]{1,0:T(8,128)(2,1)}) %all-gather.9.cloned.1.call-update) | async-done | bytes 4194320 | tf_op jit(solution)/shard_map/all_gather | solution.py:877
  240.3 11.4 %fusion.2 = (bf16[2048,704]{0,1:T(8,128)(2,1)S(1)}, bf16[2048,704]{0,1:T(8,128)(2,1)S(1)}, bf16[2048,704]{0,1:T(8,128)(2,1)}) fusion(f32[2048,1408]{0,1:T(8,128)} %fusion.6, bf16[2048,1024]{1,0:T(8,128)(2,1)} %all-gather.9.cloned.1.call-done, bf16[1024,2112]{0,1:T(8,128)(2,1)} %all-gather.7.cloned.1.call-done), kind=kOutput, calls=%fused_computation.5 | convolution fusion | flops 2977300480 | bytes 25821184 | tf_op jit(solution)/shard_map/dot_general | solution.py:22
  251.7 1.6 copy-done.10
  254.2 8.6 %convolution_convert_fusion.1 = bf16[2048,1024]{1,0:T(8,128)(2,1)} fusion(bf16[2048,704]{0,1:T(8,128)(2,1)S(1)} %get-tuple-element.144, bf16[2048,704]{0,1:T(8,128)(2,1)S(1)} %get-tuple-element.143, bf16[1024,2112]{0,1:T(8,128)(2,1)S(1)} %copy-done.9), kind=kOutput, calls=%fused_computation.12 | convolution fusion | flops 5919211520 | bytes 12845056 | tf_op jit(solution)/shard_map/dot_general | solution.py:22
  262.8 7.8 %convolution_convert_fusion.2 = bf16[2048,1024]{1,0:T(8,128)(2,1)} fusion(bf16[2048,704]{0,1:T(8,128)(2,1)} %get-tuple-element.145, bf16[1024,2112]{0,1:T(8,128)(2,1)} %all-gather.7.cloned.1.call-done), kind=kOutput, calls=%fused_computation.13 | convolution fusion | flops 2954887168 | bytes 8519680 | tf_op jit(solution)/shard_map/dot_general | solution.py:22
  270.6 12.1 %reduce-scatter.11.cloned.1.call-start = ((), (), s32[]{:S(2)}) async-start(), calls=%async_computation.11 | async-start | bytes 5013504 | tf_op jit(solution)/shard_map/reduce_scatter | solution.py:941
  282.7 7.3 %fusion.15 = bf16[1024,704]{0,1:T(8,128)(2,1)} fusion(bf16[2048,704]{0,1:T(8,128)(2,1)} %get-tuple-element.145, bf16[2048,1024]{1,0:T(8,128)(2,1)} %all-gather.9.cloned.1.call-done), kind=kOutput, calls=%fused_computation.33 | convolution fusion | flops 2953510912 | bytes 8519680 | tf_op jit(solution)/shard_map/dot_general | solution.py:22
  290.1 1.7 copy.114
  291.8 10.3 %convolution_convert_fusion = bf16[1024,1408]{1,0:T(8,128)(2,1)S(1)} fusion(bf16[2048,1024]{1,0:T(8,128)(2,1)} %all-gather.5.cloned.1.call-done, bf16[2048,704]{0,1:T(8,128)(2,1)} %copy-done.11, bf16[2048,704]{0,1:T(8,128)(2,1)} %copy-done.10), kind=kOutput, calls=%fused_computation.11 | convolution fusion | flops 5918556160 | bytes 12845056 | tf_op jit(solution)/shard_map/dot_general | solution.py:22
  302.1 2.4 pad_maximum_fusion.1
  304.5 2.9 reduce-scatter.9.cloned.1.call-done
  307.5 2.1 fusion.14
  309.6 45.0 %reduce-scatter.7.cloned.1.call-done = bf16[512,1024]{1,0:T(8,128)(2,1)} async-done(((bf16[2048,1024]{1,0:T(8,128)(2,1)}), bf16[512,1024]{1,0:T(8,128)(2,1)}) %reduce-scatter.7.cloned.1.call-update) | async-done | bytes 1048592 | tf_op jit(solution)/shard_map/reduce_scatter | solution.py:881
  354.6 4.5 fusion.27
  359.1 91.0 %reduce-scatter.11.cloned.1.call-done = bf16[128,2112]{1,0:T(8,128)(2,1)} async-done(((bf16[1024,2112]{1,0:T(8,128)(2,1)}), bf16[128,2112]{1,0:T(8,128)(2,1)}) %reduce-scatter.11.cloned.1.call-update) | async-done | bytes 540688 | tf_op jit(solution)/shard_map/reduce_scatter | solution.py:941
  454.2 45.4 %mixer_bwd.1 = (bf16[2048,1152]{1,0:T(8,128)(2,1)}, f32[4,768]{1,0:T(4,128)}, f32[1,128]{1,0:T(1,128)}) custom-call(bf16[2048,1024]{1,0:T(8,128)(2,1)} %all-gather.11.cloned.1.call-done.hg_ref, bf16[1024,1408]{1,0:T(8,128)(2,1)} %bitcast.58, f32[2048,1152]{1,0:T(8,128)} %get-tuple-element.35.pre_ref.halo_ref, ...), custom_call_target="tpu_custom_call" | custom-call | tf_op jit(solution)/shard_map/mixer_bwd/pallas_call | solution.py:334
  500.3 1.3 fusion.19.small_ref
  501.6 73.8 %end.1 = (f32[512,1024]{1,0:T(8,128)}, f32[128,1408]{1,0:T(8,128)}, f32[48,128]{1,0:T(8,128)}) custom-call(bf16[2048,1152]{1,0:T(8,128)(2,1)} %get-tuple-element.43.dpre_ref, bf16[1024,1408]{1,0:T(8,128)(2,1)} %bitcast.59, bf16[2048,1024]{1,0:T(8,128)(2,1)} %bitcast.61, bf16[2048,1024]{1,0:T(8,128)(2,1)} %all-gather.11.cloned.1.call-done.hg_ref, ...), custom_call_target="tpu_custom_call" | custom-call | tf_op jit(solution)/shard_map/end/pallas_call | solution.py:823
  575.4 2.0 slice_bitcast_fusion.1
  579.0 1.3 slice_bitcast_fusion.2
  583.4 3.2 copy.127
  (82 shorter events, 21.9 us)
Async XLA Ops:
  8.0 127.5 %reduce-scatter.5.cloned.1.call-start = ((), (), s32[]{:S(2)}) async-start(), calls=%async_computation.4 | async-start | bytes 5242880 | tf_op jit(solution)/shard_map/reduce_scatter | solution.py:881
  18.4 0.7 copy-start.4
  92.6 0.9 copy-start.5
  92.6 1.0 copy-start.6
  92.6 1.1 copy-start.7
  92.6 42.9 %copy-start = (bf16[512,1024]{1,0:T(8,128)(2,1)S(1)}, bf16[512,1024]{1,0:T(8,128)(2,1)}, u32[]{:S(2)}) copy-start(bf16[512,1024]{1,0:T(8,128)(2,1)} %tok_ref.3) | copy-start | bytes 3145732
  92.7 44.5 %copy-start.8 = (f32[1024]{0:T(1024)S(1)}, f32[1024]{0:T(1024)}, u32[]{:S(2)}) copy-start(f32[1024]{0:T(1024)} %param.27) | copy-start | bytes 12292
  92.7 77.2 %all-gather.7.cloned.1.call-start = ((), (), s32[]{:S(2)}) async-start(), calls=%async_computation.6 | async-start | bytes 4866048 | tf_op jit(solution)/shard_map/all_gather | solution.py:910
  94.6 109.9 %all-gather.5.cloned.1.call-start = ((), (), s32[]{:S(2)}) async-start(), calls=%async_computation.5 | async-start | bytes 5242880 | tf_op jit(solution)/shard_map/all_gather | solution.py:877
  139.8 100.5 %all-gather.9.cloned.1.call-start = ((), (), s32[]{:S(2)}) async-start(), calls=%async_computation.8 | async-start | bytes 5242880 | tf_op jit(solution)/shard_map/all_gather | solution.py:877
  140.4 167.1 %reduce-scatter.9.cloned.1.call-start = ((), (), s32[]{:S(2)}) async-start(), calls=%async_computation.9 | async-start | bytes 5242880 | tf_op jit(solution)/shard_map/reduce_scatter | solution.py:881
  240.3 13.9 %copy-start.9 = (bf16[1024,2112]{0,1:T(8,128)(2,1)S(1)}, bf16[1024,2112]{0,1:T(8,128)(2,1)}, u32[]{:S(2)}) copy-start(bf16[1024,2112]{0,1:T(8,128)(2,1)} %all-gather.7.cloned.1.call-done) | copy-start | bytes 12976132
  251.7 1.6 copy-start.10
  251.7 2.5 copy-start.11
  262.8 91.8 %reduce-scatter.7.cloned.1.call-start = ((), (), s32[]{:S(2)}) async-start(), calls=%async_computation.7 | async-start | bytes 5242880 | tf_op jit(solution)/shard_map/reduce_scatter | solution.py:881
  270.6 179.5 %reduce-scatter.11.cloned.1.call-start = ((), (), s32[]{:S(2)}) async-start(), calls=%async_computation.11 | async-start | bytes 5013504 | tf_op jit(solution)/shard_map/reduce_scatter | solution.py:941
  304.5 3.0 copy-start.1
  304.5 50.1 %copy-start.2 = (bf16[512,1024]{1,0:T(8,128)(2,1)S(1)}, bf16[512,1024]{1,0:T(8,128)(2,1)}, u32[]{:S(2)}) copy-start(bf16[512,1024]{1,0:T(8,128)(2,1)} %param.31) | copy-start | bytes 3145732
  304.5 149.7 %all-gather.11.cloned.1.call-start = ((), (), s32[]{:S(2)}) async-start(), calls=%async_computation.10 | async-start | bytes 5242880 | tf_op jit(solution)/shard_map/all_gather | solution.py:877
  450.1 2.1 copy-start.3
Sparse Core Ops, SparseCore 0:
  92.8 42.7 reduce-scatter.4
  262.9 44.5 reduce-scatter.8
  310.0 44.5 reduce-scatter.6
  358.5 91.6 reduce-scatter.10
Sparse Core Ops, SparseCore 1:
  95.4 74.4 all-gather.6
  171.9 32.5 all-gather.4
  206.0 34.3 all-gather.8
  359.2 34.3 all-gather.10

commit v3 on v2

--- a/solution.py
+++ b/solution.py
@@ -15,7 +15,6 @@
 F32 = jnp.float32
 BF16 = jnp.bfloat16
 VMEM_LIMIT = 56 * 1024 * 1024
-SOLVE_PASSES = 1
 
 
 def dot(left, right, dims):
@@ -32,18 +31,6 @@
 
 def t_mul(left, right):
     return dot(left.astype(BF16), right.astype(BF16), ((0,), (0,)))
-
-
-def mul_split(left, right):
-    lead_l = left.astype(BF16)
-    rest_l = (left - lead_l.astype(F32)).astype(BF16)
-    lead_r = right.astype(BF16)
-    rest_r = (right - lead_r.astype(F32)).astype(BF16)
-    dims = ((1,), (0,))
-    return dot(lead_l, lead_r, dims) + (dot(rest_l, lead_r, dims) + dot(lead_l, rest_r, dims))
-
-
-solve_mul = mul if SOLVE_PASSES == 1 else mul_split
 
 
 def unit_inverses(lowers):
@@ -57,8 +44,8 @@
     solved = [eye - jnp.where(first, a, 0.0) for a in lowers]
     for bit in range(1, CHUNK.bit_length() - 1):
         mask = level(bit)
-        right = [solve_mul(jnp.where(mask, a, 0.0), t) for a, t in zip(lowers, solved)]
-        solved = [t - solve_mul(t, r) for t, r in zip(solved, right)]
+        right = [mul(jnp.where(mask, a, 0.0), t) for a, t in zip(lowers, solved)]
+        solved = [t - mul(t, r) for t, r in zip(solved, right)]
     return solved
 
 
@@ -518,25 +505,29 @@
     )(tokens, gain, mine)
 
 
+def when(condition):
+    return pl.when(condition) if not isinstance(condition, bool) else (lambda f: f() if condition else None)
+
+
 class HeadScatter:
-    def __init__(self, count, parts, refs):
-        self.count, self.parts = count, parts
+    def __init__(self, count, refs):
+        self.count = count
         (self.out, self.near, self.onward, self.far, self.own,
          self.out_s, self.near_r, self.onward_s, self.far_r) = refs
         self.me = lax.axis_index("head")
         self.side, self.place = self.me % 2, self.me // 2
         self.pair = self.me + 1 - 2 * self.side
-        self.size = self.own.shape[0] // parts
+        self.parts, self.depth, self.size = self.near.shape[0], self.own.shape[0], self.own.shape[1]
 
     @staticmethod
-    def scratch(count, parts, rows, width):
-        size, half = rows // parts, count // 2
+    def scratch(count, parts, size, width, depth):
+        half = count // 2
         return [
             pltpu.VMEM((2, 2, half, size, width), BF16),
             pltpu.VMEM((parts, half, size, width), BF16),
             pltpu.VMEM((2, half - 1, size, width), BF16),
             pltpu.VMEM((parts, half - 1, size, width), BF16),
-            pltpu.VMEM((rows, width), F32),
+            pltpu.VMEM((depth, size, width), F32),
             pltpu.SemaphoreType.DMA((2,)),
             pltpu.SemaphoreType.DMA((parts,)),
             pltpu.SemaphoreType.DMA((2, half - 1)),
@@ -553,8 +544,7 @@
         return remote(self.onward.at[slot, f], self.far.at[p, f], self.onward_s.at[slot, f], self.far_r.at[p, f], "head", to)
 
     def offer(self, p, total):
-        if p >= 2:
-            self._near(p - 2).wait_send()
+        when(p >= 2)(lambda: self._near(p - 2).wait_send())
         for owner in range(self.count):
             self.out[p % 2, owner % 2, owner // 2] = total[owner * self.size : (owner + 1) * self.size].astype(BF16)
         self._near(p).start()
@@ -564,14 +554,13 @@
         self._near(p).wait_recv()
         both = lambda i: self.out[slot, self.side, i].astype(F32) + self.near[p, i].astype(F32)
         for f in range(half - 1):
-            if p >= 2:
-                self._far(p - 2, f).wait_send()
+            when(p >= 2)(lambda f=f: self._far(p - 2, f).wait_send())
             self.onward[slot, f] = both(lax.rem(self.place + f + 1, half)).astype(BF16)
             self._far(p, f).start()
-        self.own[p * self.size : (p + 1) * self.size, :] = both(self.place)
+        self.own[p % self.depth] = both(self.place)
 
     def take(self, p):
-        total = self.own[p * self.size : (p + 1) * self.size, :]
+        total = self.own[p % self.depth]
         for f in range(self.count // 2 - 1):
             self._far(p, f).wait_recv()
             total = total + self.far[p, f].astype(F32)
@@ -582,6 +571,195 @@
             self._near(p).wait_send()
             for f in range(self.count // 2 - 1):
                 self._far(p, f).wait_send()
+
+
+class HeadGather:
+    def __init__(self, count, parts, own, block, refs):
+        self.count, self.parts, self.own, self.block = count, parts, own, block
+        self.far_s, self.pair_s, self.fwd_s, self.got = refs
+        self.me = lax.axis_index("head")
+        self.pair = self.me + 1 - 2 * (self.me % 2)
+
+    @staticmethod
+    def scratch(count, parts):
+        far = count // 2 - 1
+        return [pltpu.SemaphoreType.DMA(s) for s in ((far, parts), (parts,), (far, parts), (count, parts))]
+
+    def _fars(self, base):
+        return [(f, lax.rem(base + 2 * (f + 1), self.count)) for f in range(self.count // 2 - 1)]
+
+    def _far(self, p, f, far):
+        return remote(self.own(p), self.block(self.me, p), self.far_s.at[f, p], self.got.at[self.me, p], "head", far)
+
+    def _pair(self, p):
+        return remote(self.own(p), self.block(self.me, p), self.pair_s.at[p], self.got.at[self.me, p], "head", self.pair)
+
+    def _on(self, p, f, owner):
+        return remote(self.block(owner, p), self.block(owner, p), self.fwd_s.at[f, p], self.got.at[owner, p], "head", self.pair)
+
+    def send(self, p):
+        for f, far in self._fars(self.me):
+            self._far(p, f, far).start()
+        self._pair(p).start()
+
+    def pass_on(self, p):
+        for f, far in self._fars(self.me):
+            self._on(p, f, far).wait_recv()
+            self._on(p, f, far).start()
+
+    def arrive(self, p):
+        remote(self.own(p), self.block(self.pair, p), self.pair_s.at[p], self.got.at[self.pair, p], "head", self.pair).wait_recv()
+        for f, far in self._fars(self.pair):
+            self._on(p, f, far).wait_recv()
+
+    def sent(self, p):
+        self._pair(p).wait_send()
+        for f, far in self._fars(self.me):
+            self._far(p, f, far).wait_send()
+            self._on(p, f, far).wait_send()
+
+
+def greet_head(count):
+    barrier = pltpu.get_barrier_semaphore()
+    me = lax.axis_index("head")
+    for to in [me + 1 - 2 * (me % 2)] + [lax.rem(me + 2 * f, count) for f in range(1, count // 2)]:
+        pl.semaphore_signal(barrier, 1, device_id={"head": to}, device_id_type=MESH)
+    pl.semaphore_wait(barrier, count // 2)
+
+
+def mid_kernel(count, parts, mixed_ref, weights_ref, tok_ref, gain_ref, cot_ref, ff_ref,
+               out_ref, grad_ref, hg_ref, gain_grad_ref, terms_ref, *scratch):
+    scratch = list(scratch)
+    take = lambda n: [scratch.pop(0) for _ in range(n)]
+    att_refs, down_refs, back_refs = take(9), take(9), take(9)
+    second_sems, hg_sems = take(4), take(4)
+    out_t, second, hidden, hg_own, total, loads, keep_s = scratch
+    size, width = tok_ref.shape[1:]
+    ff = ff_ref.shape[1] // 3
+    me = lax.axis_index("head")
+    load = pltpu.make_async_copy(weights_ref.at[:, : out_t.shape[1]], out_t, loads.at[0])
+    load.start()
+    greet_head(count)
+    att, down, back = (HeadScatter(count, r) for r in (att_refs, down_refs, back_refs))
+    here = lambda owner, p: second.at[p, owner]
+    seconds = HeadGather(count, parts, lambda p: here(me, p), here, second_sems)
+    there = lambda owner, p: hg_ref.at[owner, p]
+    hgs = HeadGather(count, parts, lambda p: hg_own.at[p], there, hg_sems)
+    keep = lambda p: pltpu.make_async_copy(hg_own.at[p], there(me, p), keep_s.at[p])
+    total[...] = jnp.zeros_like(total)
+    gain_grad_ref[...] = jnp.zeros_like(gain_grad_ref)
+    load.wait()
+
+    def within(p, stage):
+        pl.when(jnp.logical_and(p >= 0, p < parts))(lambda: stage(p))
+
+    def attend(p):
+        rows = mixed_ref[:, p].reshape(count * size, mixed_ref.shape[3])
+        att.offer(p, dot(rows, out_t[...], ((1,), (1,))))
+
+    def norm(p):
+        rows = tok_ref[p].astype(F32) + att.take(p)
+        hidden[p] = rows
+        inv = lax.rsqrt(jnp.mean(rows * rows, axis=-1, keepdims=True) + 1e-6)
+        second[p, me] = (rows * inv * gain_ref[...]).astype(BF16)
+        seconds.send(p)
+
+    def feed(p):
+        seconds.arrive(p)
+        rows = second[p].reshape(count * size, width)
+        both = dot(rows, ff_ref[:, : 2 * ff], ((1,), (0,)))
+        gate, up = both[:, :ff], both[:, ff:]
+        sig = jax.nn.sigmoid(gate)
+        act = gate * sig
+        middle = (act * up).astype(BF16)
+        down.offer(p, dot(middle, ff_ref[:, 2 * ff :], ((1,), (1,))))
+        cot = cot_ref[:, p].reshape(count * size, width)
+        grad = dot(cot, ff_ref[:, 2 * ff :], ((1,), (0,))).astype(BF16).astype(F32)
+        pair = jnp.concatenate(
+            [(grad * up * sig * (1.0 + gate * (1.0 - sig))).astype(BF16), (grad * act).astype(BF16)], axis=1
+        )
+        back.offer(p, dot(pair, ff_ref[:, : 2 * ff], ((1,), (1,))))
+        total[:, : 2 * ff] += dot(rows, pair, ((0,), (0,)))
+        total[:, 2 * ff :] += dot(cot, middle, ((0,), (0,)))
+
+    def turn(p):
+        down.turn(p)
+        back.turn(p)
+
+    def finish(p):
+        rows = hidden[p]
+        out_ref[p] = (rows + down.take(p)).astype(BF16)
+        second_grad = back.take(p).astype(BF16).astype(F32)
+        inv = lax.rsqrt(jnp.mean(rows * rows, axis=-1, keepdims=True) + 1e-6)
+        scaled = second_grad * gain_ref[...]
+        mean = jnp.mean(scaled * rows, axis=-1, keepdims=True)
+        grad = cot_ref[me, p].astype(F32) + inv * scaled - rows * (inv * inv * inv * mean)
+        grad_ref[p] = grad
+        gain_grad_ref[...] += jnp.sum(second_grad * rows * inv, axis=0, keepdims=True)
+        hg_own[p] = grad.astype(BF16)
+        hgs.send(p)
+        keep(p).start()
+
+    @pl.loop(0, parts + 4)
+    def _(step):
+        i = step - 1
+        within(i + 1, attend)
+        within(i, norm)
+        within(i + 1, att.turn)
+        within(i - 1, feed)
+        within(i, seconds.pass_on)
+        within(i - 1, turn)
+        within(i - 2, finish)
+        within(i - 3, hgs.pass_on)
+
+    terms_ref[...] = total[...].astype(BF16)
+
+    @pl.loop(0, parts)
+    def _(p):
+        hgs.arrive(p)
+        keep(p).wait()
+        hgs.sent(p)
+        seconds.sent(p)
+
+    for s in (att, down, back):
+        s.close()
+
+
+def mid(mixed, weights, tokens, gain, cot_rows, ff_set, count, parts=8):
+    rows, width = tokens.shape
+    size, hid = rows // parts, mixed.shape[1]
+    anywhere = pl.BlockSpec(memory_space=pl.ANY)
+    vmem = pl.BlockSpec(memory_space=pltpu.VMEM)
+    scatter = HeadScatter.scratch(count, parts, size, width, 2)
+    out, grad, hg, gain_grad, terms = pl.pallas_call(
+        partial(mid_kernel, count, parts),
+        out_shape=[
+            jax.ShapeDtypeStruct((parts, size, width), BF16),
+            jax.ShapeDtypeStruct((parts, size, width), F32),
+            jax.ShapeDtypeStruct((count, parts, size, width), BF16),
+            jax.ShapeDtypeStruct((1, width), F32),
+            jax.ShapeDtypeStruct(ff_set.shape, BF16),
+        ],
+        in_specs=[vmem, anywhere] + [vmem] * 4,
+        out_specs=[vmem, vmem, anywhere, vmem, vmem],
+        scratch_shapes=scatter * 3
+        + HeadGather.scratch(count, parts) * 2
+        + [
+            pltpu.VMEM((width, hid), BF16),
+            pltpu.VMEM((parts, count, size, width), BF16),
+            pltpu.VMEM((parts, size, width), F32),
+            pltpu.VMEM((parts, size, width), BF16),
+            pltpu.VMEM(ff_set.shape, F32),
+            pltpu.SemaphoreType.DMA((1,)),
+            pltpu.SemaphoreType.DMA((parts,)),
+        ],
+        compiler_params=pltpu.CompilerParams(vmem_limit_bytes=61 * 1024 * 1024, has_side_effects=True, collective_id=2),
+        name="mid",
+    )(
+        mixed.reshape(count, parts, size, hid), weights, tokens.reshape(parts, size, width), gain,
+        cot_rows.reshape(count, parts, size, width), ff_set,
+    )
+    return out.reshape(rows, width), grad.reshape(rows, width), hg.reshape(-1, width), gain_grad, terms
 
 
 class DpScatter:
@@ -749,7 +927,7 @@
         ((dpre_ref, dpre), (w_ref.at[:, hid:], w), (normed_ref, normed), (mixed_ref, mixed), (hg_ref, hg)))]
     for m in moves:
         m.start()
-    heads = HeadScatter(count, parts, head_refs)
+    heads = HeadScatter(count, head_refs)
     line = DpScatter(n_dp // 2, terms, dp_refs)
     small = SmallSum(n_dp, count, shared, small_refs)
     size = rows // parts
@@ -829,7 +1007,7 @@
         ],
         in_specs=[anywhere] * 5 + [vmem] * 4,
         out_specs=[vmem] * 3,
-        scratch_shapes=HeadScatter.scratch(count, parts, rows, width)
+        scratch_shapes=HeadScatter.scratch(count, parts, rows // parts, width, parts)
         + DpScatter.scratch(n_dp // 2, block, wide)
         + SmallSum.scratch(n_dp, count, small.shape[0], shared)
         + [pltpu.VMEM((n_dp, block, wide), BF16), like(dpre), pltpu.VMEM((width, dpre.shape[1]), BF16), like(normed_rows), like(hg_rows), like(mixed),
@@ -856,29 +1034,6 @@
     columns = before + [enter, leave] + after + [doc]
     aux = jnp.stack([c.astype(F32) for c in columns], axis=1)
     return aux, doc.astype(F32).reshape(-1, GROUP, CHUNK)
-
-
-def low(values):
-    return values.astype(BF16)
-
-
-def inverse_rms(values):
-    return lax.rsqrt(jnp.mean(values * values, axis=-1, keepdims=True) + 1e-6)
-
-
-def norm_back(grad, values, inverse, gain):
-    scaled = grad * gain
-    mean = jnp.mean(scaled * values, axis=-1, keepdims=True)
-    into = inverse * scaled - values * (inverse * inverse * inverse) * mean
-    return into, jnp.sum(grad * values * inverse, axis=0)
-
-
-def gather_rows(values):
-    return lax.all_gather(values, "head", axis=0, tiled=True)
-
-
-def scatter_rows(values):
-    return lax.psum_scatter(low(values), "head", scatter_dimension=0, tiled=True).astype(F32)
 
 
 def on_device(
@@ -900,56 +1055,36 @@
     cotangent,
 ):
     hid, heads, ff = w_query.shape[1], w_beta.shape[1], w_mlp_gate.shape[1]
+    n_dp, n_head = lax.axis_size("dp"), lax.axis_size("head")
     beta_wide = jnp.pad(w_beta, ((0, 0), (0, HEAD_DIM - heads)))
     mine = jnp.concatenate([w_out.T, w_query, w_key, w_value, w_gate_out, beta_wide], axis=1)
-    n_dp, n_head = lax.axis_size("dp"), lax.axis_size("head")
     normed_rows, first_set = start(tokens, attn_gain[None, :], mine, n_dp, n_head)
     normed_rows = normed_rows.reshape(-1, normed_rows.shape[2])
     first_set = first_set.reshape(-1, first_set.shape[2])
-    mine = jnp.concatenate([w_mlp_gate, w_mlp_up, w_down.T], axis=1)
-    second_set = lax.all_gather(mine, "dp", axis=0, tiled=True)
-    out_t = first_set[:, :hid]
-    w_ff, down_t = second_set[:, : 2 * ff], second_set[:, 2 * ff :]
-
-    x = tokens.astype(F32)
+    wide = -(-ff // 256) * 256
+    mine = jnp.concatenate(
+        [jnp.pad(w, ((0, 0), (0, wide - ff))) for w in (w_mlp_gate, w_mlp_up, w_down.T)], axis=1
+    )
+    ff_set = lax.all_gather(mine, "dp", axis=0, tiled=True)
+    cot_rows = lax.all_gather(cotangent, "head", axis=0, tiled=True)
+
     length = normed_rows.shape[0]
     aux, docrow = doc_tables(lengths[0], length)
     conv = jnp.swapaxes(conv_weight.astype(F32), 0, 1).reshape(conv_weight.shape[1], 3 * hid)
     gain = head_gain[None, :]
     pre, mixed, *saved = mixer_fwd(normed_rows, first_set, aux, docrow, conv, gain)
-    attention = scatter_rows(dot(mixed, out_t, ((1,), (1,))))
-    hidden = x + attention
-    h_inv = inverse_rms(hidden)
-    second_rows = gather_rows(low(hidden * h_inv * mlp_gain))
-    both = dot(second_rows, w_ff, ((1,), (0,)))
-    gate, up = both[:, :ff], both[:, ff:]
-    sig = jax.nn.sigmoid(gate)
-    activated = gate * sig
-    middle = low(activated * up)
-    output = low(hidden + scatter_rows(dot(middle, down_t, ((1,), (1,)))))
-
-    cot_rows = gather_rows(cotangent)
-    middle_grad = low(dot(cot_rows, down_t, ((1,), (0,)))).astype(F32)
-    up_grad = low(middle_grad * activated)
-    gate_grad = low(middle_grad * up * sig * (1.0 + gate * (1.0 - sig)))
-    ff_grad = jnp.concatenate([gate_grad, up_grad], axis=1)
-    outer = lambda left, right: dot(left, right, ((0,), (0,)))
-    second_grad = low(scatter_rows(dot(ff_grad, w_ff, ((1,), (1,))))).astype(F32)
-    mlp_terms = jnp.concatenate(
-        [low(outer(second_rows, ff_grad)), low(outer(cot_rows, middle))], axis=1
+    output, hidden_grad, hg_rows, mlp_gain_grad, mlp_terms = mid(
+        mixed, first_set, tokens, mlp_gain[None, :], cot_rows, ff_set, n_head
     )
     mlp_reduced = lax.psum_scatter(mlp_terms, "dp", scatter_dimension=0, tiled=True).astype(F32)
-    from_mlp, mlp_gain_grad = norm_back(second_grad, hidden, h_inv, mlp_gain)
-    hidden_grad = cotangent.astype(F32) + from_mlp
-    hg_rows = gather_rows(low(hidden_grad))
     dpre, conv_part, head_gain_grad = mixer_bwd(
         hg_rows, first_set, aux, docrow, conv, gain, (pre, *saved)
     )
     taps = conv_part.shape[0]
-    shared = 2 * (x.shape[1] // 128) + 8
+    shared = 2 * (tokens.shape[1] // 128) + 8
     small = jnp.concatenate(
         [
-            jnp.zeros((x.shape[1] // 128, 128), F32),
+            jnp.zeros((tokens.shape[1] // 128, 128), F32),
             mlp_gain_grad.reshape(-1, 128),
             jnp.pad(head_gain_grad, ((0, 7), (0, 0))),
             conv_part.reshape(-1, 128),
@@ -976,8 +1111,8 @@
         mix_reduced[:, :hid].T,
         gains[1],
         mlp_reduced[:, :ff],
-        mlp_reduced[:, ff : 2 * ff],
-        mlp_reduced[:, 2 * ff :].T,
+        mlp_reduced[:, wide : wide + ff],
+        mlp_reduced[:, 2 * wide : 2 * wide + ff].T,
     )
 
 

time: 602 us -> 440 us (0.73)
  waiting for transfers between devices: 268 us -> 54.8 us
  Pallas kernels: 188 us -> 345 us
  matrix products: 61.5 us -> 0 us
  other arithmetic: 19.7 us -> 5.03 us
  starting transfers between devices: 12.7 us -> 0.12 us
  local copies, waits for them, and re-layouts: 28 us -> 17.5 us
    pallas_call x0 -> x1, Pallas kernels: none -> 133 us  [mid(): pl.pallas_call(partial(mid_kernel, count, parts), out_shape=[jax.ShapeDty...]
    reduce_scatter x1, waiting for transfers between devices: 91 us -> 0.01 us  [on_device(): lax.psum_scatter(mlp_terms, 'dp', scatter_dimension=0, tiled=True)]
    reduce_scatter x3 -> x0, waiting for transfers between devices: 88.8 us -> none  [scatter_rows(): lax.psum_scatter(low(values), 'head', scatter_dimension=0, tiled=True)]
    dot_general x7 -> x0, matrix products: 61.5 us -> none  [dot(): lax.dot_general(left, right, (dims, ((), ())), preferred_element_type=F32)]
    all_gather x4 -> x2, waiting for transfers between devices: 88 us -> 54.1 us  [the longest x1 54.1 us: on_device(): ff_set = lax.all_gather(mine, 'dp', axis=0, tiled=True)]
    pallas_call x1, Pallas kernels: 41.1 us -> 53.3 us  [start(): pl.pallas_call(partial(start_kernel, lines, n_head, parts), out_shape=[ja...]
    reduce_scatter x1, starting transfers between devices: 12.1 us -> 0.04 us  [on_device(): lax.psum_scatter(mlp_terms, 'dp', scatter_dimension=0, tiled=True)]
    pallas_call x1, Pallas kernels: 73.8 us -> 85.2 us  [end(): pl.pallas_call(partial(end_kernel, n_dp, count, parts, shared), out_shape...]
  transfers between devices with their start and end apart: 8 -> 3, of which waited for: 7 -> 1; matrix products, arithmetic and copies ran while one was open for 10% -> 3% of each run, Pallas kernels for 0% -> 49%
where the time goes in v3:
time: 440 us; the launch traced here: 436 us
  Pallas kernels  345 us (78%)
  waiting for transfers between devices  54.8 us (12%)
  local copies, waits for them, and re-layouts  17.5 us (4%)
  between operations  14.3 us (3%)
  other arithmetic  5.03 us (1%)
    pallas_call x1, Pallas kernels, mid(): pl.pallas_call(partial(mid_kernel, count, parts), out_shape=[jax.ShapeDty...  133 us
    pallas_call x1, Pallas kernels, end(): pl.pallas_call(partial(end_kernel, n_dp, count, parts, shared), out_shape...  85.2 us
    all_gather x1, waiting for transfers between devices, on_device(): ff_set = lax.all_gather(mine, 'dp', axis=0, tiled=True)  54.1 us
    pallas_call x1, Pallas kernels, start(): pl.pallas_call(partial(start_kernel, lines, n_head, parts), out_shape=[ja...  53.3 us
    pallas_call x1, Pallas kernels, mixer_bwd(): pl.pallas_call(mixer_bwd_kernel, grid=(steps,), in_specs=[rows(hg_rows.sh...  45.6 us
    pallas_call x1, Pallas kernels, mixer_fwd(): pl.pallas_call(mixer_fwd_kernel, grid=(length // STEP,), in_specs=[rows(x...  27.8 us
    unnamed x50, local copies, waits for them, and re-layouts  10.5 us
  transfers between devices with their start and end apart: 3, of which 1 were waited for; matrix products, arithmetic and copies ran while one was open for 3% of the time, Pallas kernels for 49%

profile of v3, /device:TPU:0, one launch (start us, length us, event | category | flops | bytes accessed | tf_op | source)
XLA Modules:
  0.0 436.3 jit_solution(2311693265436104812)
XLA Ops:
  7.2 0.7 all-gather.3.cloned.1.call-update
  8.0 1.1 copy.111
  9.1 0.1 copy.109
  9.2 0.1 copy.110
  9.4 0.9 fusion.5
  10.6 0.6 convert_element_type.82
  11.5 0.2 slice_reduce_fusion
  12.3 1.3 copy.108.aux_ref
  13.9 0.6 reshape.211
  14.7 0.7 copy-done.3
  15.4 53.3 %start.1 = (bf16[4,512,1024]{2,1,0:T(8,128)(2,1)}, bf16[8,128,1408]{2,1,0:T(8,128)(2,1)}) custom-call(bf16[512,1024]{1,0:T(8,128)(2,1)} %tok_ref.3, f32[1,1024]{1,0:T(1,128)} %bitcast.74, bf16[128,1408]{1,0:T(8,128)(2,1)} %copy-done.3), custom_call_target="tpu_custom_call" | custom-call | tf_op jit(solution)/shard_map/start/pallas_call | solution.py:492
  68.7 27.8 %mixer_fwd.1 = (f32[2048,1152]{1,0:T(8,128)}, bf16[2048,256]{1,0:T(8,128)(2,1)}, f32[2048,256]{1,0:T(8,128)}, bf16[16,2,128,128]{3,2,1,0:T(8,128)(2,1)}, bf16[16...) custom-call(bf16[2048,1024]{1,0:T(8,128)(2,1)} %bitcast.49, ...), custom_call_target="tpu_custom_call" | custom-call | tf_op jit(solution)/shard_map/mixer_fwd/pallas_call | solution.py:286
  96.5 54.1 %all-gather.5.cloned.1.call-done.ff_ref = bf16[1024,2304]{1,0:T(8,128)(2,1)} async-done(((bf16[128,2304]{1,0:T(8,128)(2,1)}), bf16[1024,2304]{1,0:T(8,128)(2,1)}) %all-gather.5.cloned.1.call-update) | async-done | bytes 4718608 | tf_op jit(solution)/shard_map/all_gather | solution.py:1068
  150.6 132.7 %mid.1 = (bf16[8,64,1024]{2,1,0:T(8,128)(2,1)}, f32[8,64,1024]{2,1,0:T(8,128)}, bf16[4,8,64,1024]{3,2,1,0:T(8,128)(2,1)}, f32[1,1024]{1,0:T(1,128)}, bf16[1024,2304]{1,0:T(8,128)(2,1)}) custom-call(bf16[4,8,64,256]{3,2,1,0:T(8,128)(2,1)} %bitcast.52, bf16[1024,1408]{1,0:T(8,128)(2,1)} %bitcast.44, bf16[8,64,1024]{2,1,0:T(8,128)(2,1)} %bitcast.51, ...), custom_call_target="tpu_custom_call" | custom-call | tf_op jit(solution)/shard_map/mid/pallas_call | solution.py:734
  283.4 45.6 %mixer_bwd.1 = (bf16[2048,1152]{1,0:T(8,128)(2,1)}, f32[4,768]{1,0:T(4,128)}, f32[1,128]{1,0:T(1,128)}) custom-call(bf16[2048,1024]{1,0:T(8,128)(2,1)} %bitcast.47, bf16[1024,1408]{1,0:T(8,128)(2,1)} %bitcast.45, f32[2048,1152]{1,0:T(8,128)} %get-tuple-element.42.pre_ref.halo_ref, f32[2048,1152]{1,0:T(8,128)} %get-tuple-element.42.pre_ref.halo_ref, ...), custom_call_target="tpu_custom_call" | custom-call | tf_op jit(solution)/shard_map/mixer_bwd/pallas_call | solution.py:321
  329.0 0.7 reshape.203
  329.7 1.3 fusion.6.small_ref
  331.0 85.2 %end.1 = (f32[512,1024]{1,0:T(8,128)}, f32[128,1408]{1,0:T(8,128)}, f32[48,128]{1,0:T(8,128)}) custom-call(bf16[2048,1152]{1,0:T(8,128)(2,1)} %get-tuple-element.50.dpre_ref, bf16[1024,1408]{1,0:T(8,128)(2,1)} %bitcast.46, bf16[2048,1024]{1,0:T(8,128)(2,1)} %bitcast.50, bf16[2048,1024]{1,0:T(8,128)(2,1)} %bitcast.48, ...), custom_call_target="tpu_custom_call" | custom-call | tf_op jit(solution)/shard_map/end/pallas_call | solution.py:1001
  416.2 0.9 slice.81
  417.1 2.0 slice_bitcast_fusion.1
  419.0 0.8 copy.115
  419.8 0.6 copy.113
  420.5 0.6 copy.114
  421.1 0.5 slice_bitcast_fusion.4
  421.6 0.6 slice_bitcast_fusion.2
  422.2 1.1 convert_element_type.84
  423.4 0.9 copy.118
  424.4 0.9 copy.116
  425.3 0.9 copy.117
  426.3 1.0 copy.126
  427.2 1.0 copy-done.1
  428.2 1.3 copy.127
  (65 shorter events, 1.9 us)
Async XLA Ops:
  7.2 1.9 copy-start.4
  7.2 2.0 copy-start.5
  7.2 89.3 %all-gather.3.cloned.1.call-start = ((), (), s32[]{:S(2)}) async-start(), calls=%async_computation.1 | async-start | bytes 5242880 | tf_op jit(solution)/shard_map/all_gather | solution.py:1069
  7.9 142.7 %all-gather.5.cloned.1.call-start = ((), (), s32[]{:S(2)}) async-start(), calls=%async_computation.2 | async-start | bytes 5308416 | tf_op jit(solution)/shard_map/all_gather | solution.py:1068
  9.1 1.3 copy-start.15
  10.3 3.4 copy-start.6
  10.3 3.5 copy-start.14
  10.3 3.6 copy-start.12
  10.3 4.2 copy-start.7
  10.3 4.2 copy-start.8
  10.3 4.3 copy-start.9
  10.3 411.8 %reduce-scatter.2.cloned.1.call-start = ((), (), s32[]{:S(2)}) async-start(), calls=%async_computation.3 | async-start | bytes 5308416 | tf_op jit(solution)/shard_map/reduce_scatter | solution.py:1079
  11.7 2.9 copy-start.10
  14.6 0.7 copy-start.3
  283.4 46.3 %copy-start.13 = (f32[1,1024]{1,0:T(1,128)S(1)}, f32[1,1024]{1,0:T(1,128)}, u32[]{:S(2)}) copy-start(f32[1,1024]{1,0:T(1,128)} %get-tuple-element.52) | copy-start | bytes 12292
  416.2 4.2 copy-start.11
  423.3 1.1 copy-start
  424.4 1.9 copy-start.2
  426.2 2.0 copy-start.1
Sparse Core Ops, SparseCore 0:
  9.6 58.6 all-gather.2
  70.5 80.0 all-gather.4
  283.5 106.4 reduce-scatter.1
